TPU v7x, 32 devices: a whole 2x2x4 slice. The times are simulated.
32 devices in a mesh: groups: 2 (over y), ctx: 8 (over z, core), rep: 2 (over x), row: 1.
Axes of the slice: x: 2, y: 2, z: 4, core: 2. Of those that a mesh axis runs over, the one named last changes fastest.
Arguments:
- queries: bfloat16 [4, 128, 64, 128], P(None, ('groups', 'ctx', 'row'), 'rep'), parts along dimension 1, may hold values from -8 to 8
- new_keys: bfloat16 [4, 128, 8, 128], P(None, ('groups', 'ctx', 'row'), 'rep'), parts along dimension 1, may hold values from -4.5 to 4.5
- step_new_values: bfloat16 [4, 128, 8, 128], P(None, ('groups', 'ctx', 'row'), 'rep'), parts along dimension 1, may hold values from -6 to 6
- context_keys: bfloat16 [8, 8192, 128], P('rep', ('groups', 'ctx')), parts along dimension 1, may hold values from -6 to 6
- context_values: bfloat16 [8, 8192, 128], P('rep', ('groups', 'ctx')), parts along dimension 1, may hold values from -6 to 6
- cluster_centroid_keys: bfloat16 [8, 64, 128], P('rep', ('groups', 'ctx')), parts along dimension 1, may hold values from -4 to 4
- cluster_mean_values: bfloat16 [8, 64, 128], P('rep', ('groups', 'ctx')), parts along dimension 1, may hold values from -6 to 6
- cluster_page_slot: int32 [8, 64], P('rep', 'groups'), parts along dimension 1, may hold values from 0 to 31, each once within a row
- picks: int32 [128, 8, 16], P(('groups', 'ctx', 'row'), 'rep'), parts along dimension 0, may hold values from 0 to 31, all different within a row
Outputs:
- attention: bfloat16 [4, 128, 64, 128], P(None, ('groups', 'ctx', 'row'), 'rep'), parts along dimension 1
There are 2 independent parts, one for each index of `groups`. A program takes and returns all parts, laid end to end along the dimension named above; each array names one. Nothing has to cross between parts.
Inputs may be any that keep to these rules, and one draw needn't show every extreme that they name: `picks`: for each row and key-value head, 16 different cluster ids. `cluster_page_slot`: for each key-value head, every cluster has its own page slot; slot p lies on context shard p // 4.
All inputs are finite; a program needn't handle non-finite values.
Results may differ from a plain program's by a relative error of at most 0.0027.
Values may be sent and summed in bfloat16 or wider, within the bound.
A program may use at most 64 MiB of HBM per device.

v0:
```python
import math

import jax
import jax.numpy as jnp
from jax import lax
from jax.sharding import PartitionSpec as P

FLOOR_SCORE = -10000.0


def tail_block(queries, new_keys, step_new_values, logit_multiplier):
    num_steps, num_rows, num_heads, head_width = queries.shape
    kv_heads = new_keys.shape[2]
    grouped = queries.astype(jnp.float32).reshape(
        num_steps, num_rows, kv_heads, num_heads // kv_heads, head_width
    )
    scores = (
        jnp.einsum("srhgd,trhd->srhgt", grouped, new_keys.astype(jnp.float32)) * logit_multiplier
    )
    step_ids = jnp.arange(num_steps, dtype=jnp.int32)
    causal = (step_ids[None, :] <= step_ids[:, None])[:, None, None, None, :]
    block_top = jnp.max(jnp.where(causal, scores, FLOOR_SCORE), axis=-1)
    weights = jnp.where(causal, jnp.exp(scores - block_top[..., None]), 0.0)
    sum_total = jnp.sum(weights, axis=-1)
    rounded = weights.astype(jnp.bfloat16).astype(jnp.float32)
    tail_out = jnp.einsum("srhgt,trhd->srhgd", rounded, step_new_values.astype(jnp.float32))
    return (
        tail_out.reshape(num_steps, num_rows, num_heads, head_width),
        sum_total.reshape(num_steps, num_rows, num_heads),
        block_top.reshape(num_steps, num_rows, num_heads),
    )


def per_device(
    queries,
    new_keys,
    step_new_values,
    context_keys,
    context_values,
    cluster_centroid_keys,
    cluster_mean_values,
    cluster_page_slot,
    picks,
):
    num_steps = queries.shape[0]
    num_heads = queries.shape[2]
    head_width = queries.shape[3]
    kv_local = context_keys.shape[0]
    span_tokens = context_keys.shape[1]
    cl_local = cluster_centroid_keys.shape[1]
    grouping_member_entries = span_tokens // cl_local
    query_group_size = num_heads // kv_local
    logit_multiplier = 1.0 / math.sqrt(head_width)
    membership_log_weight = math.log(grouping_member_entries)
    shard_index = lax.axis_index("ctx")
    gathered = lax.all_gather(queries, "ctx", axis=1, tiled=True)
    chosen = lax.all_gather(picks, "ctx", axis=0, tiled=True)
    rows_all = gathered.shape[1]
    cluster_ids = jnp.arange(cluster_page_slot.shape[1], dtype=jnp.int32)
    pick_hits = chosen[..., None] == cluster_ids
    picked_slots = jnp.sum(jnp.where(pick_hits, cluster_page_slot[None, :, None, :], 0), axis=-1)
    local_ids = shard_index * cl_local + jnp.arange(cl_local, dtype=jnp.int32)
    slot_used = jnp.any(picked_slots[..., None] == local_ids, axis=2)
    cluster_used = jnp.any(chosen[..., None] == local_ids, axis=2)
    step_outs, step_totals, step_tops = ([], [], [])
    for step_index in range(num_steps):
        head_outs, head_totals, head_tops = ([], [], [])
        for current_head_index in range(kv_local):
            generation_probe_vectors = gathered[
                step_index,
                :,
                current_head_index * query_group_size : (current_head_index + 1) * query_group_size,
                :,
            ].reshape(rows_all * query_group_size, head_width)
            exact_mask = slot_used[:, current_head_index][:, None, :, None]
            coarse_mask = jnp.logical_not(cluster_used[:, current_head_index])[:, None, :]
            exact_scores = (
                jnp.einsum(
                    "qd,kd->qk",
                    generation_probe_vectors,
                    context_keys[current_head_index],
                    preferred_element_type=jnp.float32,
                )
                * logit_multiplier
            )
            exact_scores = exact_scores.reshape(
                rows_all, query_group_size, cl_local, grouping_member_entries
            )
            prototype_logits = (
                jnp.einsum(
                    "qd,kd->qk",
                    generation_probe_vectors,
                    cluster_centroid_keys[current_head_index],
                    preferred_element_type=jnp.float32,
                )
                * logit_multiplier
                + membership_log_weight
            )
            prototype_logits = prototype_logits.reshape(rows_all, query_group_size, cl_local)
            block_top = jnp.maximum(
                jnp.max(jnp.where(exact_mask, exact_scores, FLOOR_SCORE), axis=(2, 3)),
                jnp.max(jnp.where(coarse_mask, prototype_logits, FLOOR_SCORE), axis=2),
            )
            exact_weights = jnp.where(
                exact_mask, jnp.exp(exact_scores - block_top[:, :, None, None]), 0.0
            )
            coarse_weights = jnp.where(
                coarse_mask, jnp.exp(prototype_logits - block_top[:, :, None]), 0.0
            )
            sum_total = jnp.sum(exact_weights, axis=(2, 3)) + jnp.sum(coarse_weights, axis=2)
            block_out = jnp.dot(
                exact_weights.astype(jnp.bfloat16).reshape(
                    rows_all * query_group_size, span_tokens
                ),
                context_values[current_head_index],
                preferred_element_type=jnp.float32,
            )
            block_out = block_out + jnp.dot(
                coarse_weights.astype(jnp.bfloat16).reshape(rows_all * query_group_size, cl_local),
                cluster_mean_values[current_head_index],
                preferred_element_type=jnp.float32,
            )
            head_outs.append(block_out.reshape(rows_all, query_group_size, head_width))
            head_totals.append(sum_total)
            head_tops.append(block_top)
        step_outs.append(jnp.concatenate(head_outs, axis=1))
        step_totals.append(jnp.concatenate(head_totals, axis=1))
        step_tops.append(jnp.concatenate(head_tops, axis=1))
    partial_outs = jnp.stack(step_outs)
    partial_totals = jnp.stack(step_totals)
    partial_tops = jnp.stack(step_tops)
    got_tops, got_totals, got_outs = (
        lax.all_to_all(partial_tops[None], "ctx", split_axis=2, concat_axis=0, tiled=True),
        lax.all_to_all(partial_totals[None], "ctx", split_axis=2, concat_axis=0, tiled=True),
        lax.all_to_all(partial_outs[None], "ctx", split_axis=2, concat_axis=0, tiled=True),
    )
    best_top = jnp.max(got_tops, axis=0)
    factor = jnp.exp(got_tops - best_top)
    sum_total = jnp.sum(factor * got_totals, axis=0)
    merged = jnp.sum(factor[..., None] * got_outs, axis=0)
    tail_out, tail_total, tail_top = tail_block(
        queries, new_keys, step_new_values, logit_multiplier
    )
    overall = jnp.maximum(best_top, tail_top)
    context_factor = jnp.exp(best_top - overall)
    tail_factor = jnp.exp(tail_top - overall)
    numer = context_factor[..., None] * merged + tail_factor[..., None] * tail_out
    denom = context_factor * sum_total + tail_factor * tail_total
    return (numer / denom[..., None]).astype(jnp.bfloat16)


def solution(mesh):
    return jax.shard_map(
        per_device,
        mesh=mesh,
        in_specs=(
            P(None, ("groups", "ctx", "row"), "rep", None),
            P(None, ("groups", "ctx", "row"), "rep", None),
            P(None, ("groups", "ctx", "row"), "rep", None),
            P("rep", ("groups", "ctx"), None),
            P("rep", ("groups", "ctx"), None),
            P("rep", ("groups", "ctx"), None),
            P("rep", ("groups", "ctx"), None),
            P("rep", "groups"),
            P(("groups", "ctx", "row"), "rep", None),
        ),
        out_specs=P(None, ("groups", "ctx", "row"), "rep", None),
        check_vma=False,
    )
```

profile of v0, /device:TPU:1, one launch (start us, length us, event | category | flops | bytes accessed | tf_op | source)
XLA Modules:
  0.0 259.8 jit_solution(14076466571242016807)
XLA Ops:
  7.3 15.8 %all_gather.6 = s32[64,4,16]{2,1,0:T(4,128)S(1)} all-gather(s32[8,4,16]{2,1,0:T(4,128)} %param.17), channel_id=1, replica_groups=mesh['groups'=2,'ctx'=8,'rep'=2,'row'=1] {'ctx'}, dimensions={0}, use_global_device_ids=true | all-gather | bytes 18432 | tf_op jit(solution)/shard_map/all_gather | solution.py:57
  28.6 12.0 %all-gather.2.cloned.1.call-done = bf16[4,64,32,128]{3,2,1,0:T(8,128)(2,1)} async-done(((bf16[4,8,32,128]{3,2,1,0:T(8,128)(2,1)}), bf16[4,64,32,128]{3,2,1,0:T(8,128)(2,1)}) %all-gather.2.cloned.1.call-update) | async-done | bytes 2097168 | tf_op jit(solution)/shard_map/all_gather | solution.py:56
  43.8 1.2 convolution_multiply_fusion.3
  45.0 1.2 convolution_multiply_fusion.7
  46.2 1.2 convolution_multiply_fusion.11
  47.4 1.7 select_reduce_fusion.33
  49.1 1.5 select_reduce_fusion.15
  51.9 1.4 fusion.33
  58.6 1.2 convolution_multiply_fusion.2
  59.8 1.2 convolution_multiply_fusion.6
  61.0 1.2 convolution_multiply_fusion.10
  62.2 1.7 select_reduce_fusion.32
  63.9 1.4 select_reduce_fusion.14
  66.6 1.4 fusion.35
  69.2 1.4 max.248
  70.5 1.4 max.240
  71.9 1.4 max.264
  73.3 1.4 max.256
  74.6 1.2 fusion.18
  78.0 1.2 convolution_multiply_fusion.1
  79.3 1.2 convolution_multiply_fusion.5
  84.9 1.3 fusion.37
  92.9 1.4 fusion.39
  95.6 1.4 max.252
  97.0 1.4 max.244
  98.3 1.4 max.268
  99.7 1.4 max.260
  101.1 1.3 max.250
  102.4 1.4 max.242
  103.8 1.4 max.266
  105.1 1.3 max.258
  107.3 1.7 fusion.9
  109.0 1.7 fusion.13
  110.7 1.7 fusion.1
  117.0 1.4 fusion.212
  118.4 1.7 fusion.11
  120.1 1.7 fusion.15
  124.6 1.7 fusion.12
  126.3 1.7 fusion.16
  132.1 4.1 %all-to-all-start.2 = ((f32[8,1,1024]{2,1,0:T(1,128)}), f32[8,1,1024]{2,1,0:T(1,128)}, u32[]{:S(2)}, u32[]{:S(2)}) async-start(f32[8,1,1024]{2,1,0:T(1,128)} %reshape.821), calls=%async_computation.2 | async-start | bytes 65536 | tf_op jit(solution)/shard_map/all_to_all | solution.py:134
  141.3 4.0 %all-to-all-start = ((f32[8,1,1024]{2,1,0:T(1,128)}), f32[8,1,1024]{2,1,0:T(1,128)S(1)}, u32[]{:S(2)}, u32[]{:S(2)}) async-start(f32[8,1,1024]{2,1,0:T(1,128)} %reshape.819), calls=%async_computation | async-start | bytes 65536 | tf_op jit(solution)/shard_map/all_to_all | solution.py:133
  145.3 3.7 %maximum_bitcast_fusion = f32[1,4,64,32,128]{4,3,1,0,2:T(8,128)} fusion(f32[1,64,32,128]{3,2,0,1:T(8,128)S(1)} %maximum_bitcast_fusion.4, f32[1,64,32,128]{3,2,0,1:T(8,128)} %maximum_bitcast_fusion.3, f32[1,64,32,128]{3,2,0,1:T(8,128)S(1)} %maximum_bitcast_fusion.2, f32[1,64,32,128]{3,2,0,1:T(8,128)S(1)} %maximum_bitcast_fusion.1), kind=kLoop, calls=%fused_computation | loop fusion | flops 3145728 | bytes 8388608 | tf_op jit(solution)/shard_map/broadcast_in_dim | solution.py:135
  149.0 1.3 all-to-all-done
  150.3 5.2 %all-to-all-start.1 = ((f32[1,4,64,32,128]{4,3,1,0,2:T(8,128)}), f32[1,4,64,32,128]{4,3,1,0,2:T(8,128)}, u32[]{:S(2)}, u32[]{:S(2)}) async-start(f32[1,4,64,32,128]{4,3,1,0,2:T(8,128)} %maximum_bitcast_fusion), calls=%async_computation.1 | async-start | bytes 8388608 | tf_op jit(solution)/shard_map/all_to_all | solution.py:135
  155.6 1.3 select_reduce_fusion.17
  159.1 1.5 reduce.65
  160.9 87.9 %all-to-all-done.1 = f32[1,4,64,32,128]{4,3,1,0,2:T(8,128)} async-done(((f32[1,4,64,32,128]{4,3,1,0,2:T(8,128)}), f32[1,4,64,32,128]{4,3,1,0,2:T(8,128)}, u32[]{:S(2)}, u32[]{:S(2)}) %all-to-all-start.1) | async-done | bytes 4194336 | tf_op jit(solution)/shard_map/all_to_all | solution.py:135
  248.8 2.9 %multiply_reduce_fusion = f32[4,8,32,128]{3,2,0,1:T(8,128)S(1)} fusion(f32[8,4,8,32,128]{4,3,1,2,0:T(8,128)} %bitcast.79, f32[8,4,8,32]{3,1,2,0:T(4,128)S(1)} %get-tuple-element.75), kind=kLoop, calls=%fused_computation.1 | loop fusion | flops 1966080 | bytes 4751360 | tf_op jit(solution)/shard_map/reduce_sum | solution.py:140
  (358 shorter events, 52.8 us)
Async XLA Ops:
  6.5 150.8 %copy-start = (bf16[4,8,4,128]{3,2,1,0:T(4,128)(2,1)S(1)}, bf16[4,8,4,128]{3,2,1,0:T(4,128)(2,1)}, u32[]{:S(2)}) copy-start(bf16[4,8,4,128]{3,2,1,0:T(4,128)(2,1)} %param.11) | copy-start | bytes 98308
  6.5 34.0 %copy-start.95 = (bf16[4,4,128]{2,1,0:T(4,128)(2,1)S(1)}, bf16[4,4,128]{2,1,0:T(4,128)(2,1)}, u32[]{:S(2)}) copy-start(bf16[4,4,128]{2,1,0:T(4,128)(2,1)} %param.14) | copy-start | bytes 12292
  6.5 34.0 %all-gather.2.cloned.1.call-start = ((), (), s32[]{:S(2)}) async-start(), calls=%async_computation.3 | async-start | bytes 2359296 | tf_op jit(solution)/shard_map/all_gather | solution.py:56
  23.2 20.6 %copy-start.1 = (bf16[4,512,128]{2,1,0:T(8,128)(2,1)S(1)}, bf16[4,512,128]{2,1,0:T(8,128)(2,1)}, u32[]{:S(2)}) copy-start(bf16[4,512,128]{2,1,0:T(8,128)(2,1)} %param.12) | copy-start | bytes 1572868
  50.6 9.2 %copy-start.35 = (f32[512]{0:T(512)}, f32[512]{0:T(512)S(1)}, u32[]{:S(2)}) copy-start(f32[512]{0:T(512)S(1)} %max.245) | copy-start | bytes 6148
  94.3 12.9 %copy-start.6 = (f32[512,128]{1,0:T(8,128)S(1)}, f32[512,128]{1,0:T(8,128)}, u32[]{:S(2)}) copy-start(f32[512,128]{1,0:T(8,128)} %fusion.79) | copy-start | bytes 786436
  94.3 19.7 %copy-start.7 = (f32[512,128]{1,0:T(8,128)S(1)}, f32[512,128]{1,0:T(8,128)}, u32[]{:S(2)}) copy-start(f32[512,128]{1,0:T(8,128)} %fusion.77) | copy-start | bytes 786436
  95.5 17.9 %copy-start.83 = (f32[512]{0:T(512)S(1)}, f32[512]{0:T(512)}, u32[]{:S(2)}) copy-start(f32[512]{0:T(512)} %get-tuple-element.6) | copy-start | bytes 6148
  95.5 18.1 %copy-start.81 = (f32[512]{0:T(512)S(1)}, f32[512]{0:T(512)}, u32[]{:S(2)}) copy-start(f32[512]{0:T(512)} %get-tuple-element.5) | copy-start | bytes 6148
  95.5 18.2 %copy-start.80 = (f32[512]{0:T(512)S(1)}, f32[512]{0:T(512)}, u32[]{:S(2)}) copy-start(f32[512]{0:T(512)} %get-tuple-element.7) | copy-start | bytes 6148
  95.5 18.3 %copy-start.78 = (f32[512]{0:T(512)S(1)}, f32[512]{0:T(512)}, u32[]{:S(2)}) copy-start(f32[512]{0:T(512)} %get-tuple-element.8) | copy-start | bytes 6148
  95.5 18.4 %copy-start.37 = (f32[512]{0:T(512)S(1)}, f32[512]{0:T(512)}, u32[]{:S(2)}) copy-start(f32[512]{0:T(512)} %copy-done.36) | copy-start | bytes 6148
  95.5 18.4 %copy-start.43 = (f32[512]{0:T(512)S(1)}, f32[512]{0:T(512)}, u32[]{:S(2)}) copy-start(f32[512]{0:T(512)} %copy-done.42) | copy-start | bytes 6148
  95.5 18.4 %copy-start.45 = (f32[512]{0:T(512)S(1)}, f32[512]{0:T(512)}, u32[]{:S(2)}) copy-start(f32[512]{0:T(512)} %copy-done.44) | copy-start | bytes 6148
  95.5 18.4 %copy-start.50 = (f32[512]{0:T(512)S(1)}, f32[512]{0:T(512)}, u32[]{:S(2)}) copy-start(f32[512]{0:T(512)} %copy-done.49) | copy-start | bytes 6148
  95.5 18.4 %copy-start.60 = (f32[512,4]{0,1:T(4,128)S(1)}, f32[512,4]{0,1:T(4,128)}, u32[]{:S(2)}) copy-start(f32[512,4]{0,1:T(4,128)} %copy-done.59) | copy-start | bytes 24580
  95.5 18.4 %copy-start.64 = (f32[512,4]{0,1:T(4,128)S(1)}, f32[512,4]{0,1:T(4,128)}, u32[]{:S(2)}) copy-start(f32[512,4]{0,1:T(4,128)} %copy-done.63) | copy-start | bytes 24580
  95.5 18.4 %copy-start.68 = (f32[512,4]{0,1:T(4,128)S(1)}, f32[512,4]{0,1:T(4,128)}, u32[]{:S(2)}) copy-start(f32[512,4]{0,1:T(4,128)} %copy-done.67) | copy-start | bytes 24580
  95.6 18.4 %copy-start.69 = (f32[512,4]{0,1:T(4,128)S(1)}, f32[512,4]{0,1:T(4,128)}, u32[]{:S(2)}) copy-start(f32[512,4]{0,1:T(4,128)} %get-tuple-element.91) | copy-start | bytes 24580
  95.6 18.5 %copy-start.57 = (bf16[4,4,128]{2,1,0:T(4,128)(2,1)S(1)}, bf16[4,4,128]{2,1,0:T(4,128)(2,1)}, u32[]{:S(2)}) copy-start(bf16[4,4,128]{2,1,0:T(4,128)(2,1)} %param.15) | copy-start | bytes 12292
  108.9 7.6 %copy-start.85 = (f32[512]{0:T(512)S(1)}, f32[512]{0:T(512)}, u32[]{:S(2)}) copy-start(f32[512]{0:T(512)} %get-tuple-element.10) | copy-start | bytes 6148
  108.9 7.7 %copy-start.84 = (f32[512]{0:T(512)S(1)}, f32[512]{0:T(512)}, u32[]{:S(2)}) copy-start(f32[512]{0:T(512)} %get-tuple-element.9) | copy-start | bytes 6148
  108.9 7.8 %copy-start.82 = (f32[512]{0:T(512)S(1)}, f32[512]{0:T(512)}, u32[]{:S(2)}) copy-start(f32[512]{0:T(512)} %get-tuple-element.11) | copy-start | bytes 6148
  108.9 7.9 %copy-start.79 = (f32[512]{0:T(512)S(1)}, f32[512]{0:T(512)}, u32[]{:S(2)}) copy-start(f32[512]{0:T(512)} %get-tuple-element.12) | copy-start | bytes 6148
  108.9 9.4 %copy-start.8 = (f32[512,128]{1,0:T(8,128)S(1)}, f32[512,128]{1,0:T(8,128)}, u32[]{:S(2)}) copy-start(f32[512,128]{1,0:T(8,128)} %fusion.75) | copy-start | bytes 786436
  110.7 9.4 %copy-start.4 = (f32[512,128]{1,0:T(8,128)S(1)}, f32[512,128]{1,0:T(8,128)}, u32[]{:S(2)}) copy-start(f32[512,128]{1,0:T(8,128)} %fusion.67) | copy-start | bytes 786436
  112.4 9.4 %copy-start.5 = (f32[512,128]{1,0:T(8,128)S(1)}, f32[512,128]{1,0:T(8,128)}, u32[]{:S(2)}) copy-start(f32[512,128]{1,0:T(8,128)} %fusion.91) | copy-start | bytes 786436
  113.5 9.3 %copy-start.39 = (f32[512]{0:T(512)S(1)}, f32[512]{0:T(512)}, u32[]{:S(2)}) copy-start(f32[512]{0:T(512)} %copy-done.38) | copy-start | bytes 6148
  115.0 9.6 %copy-start.11 = (f32[512,128]{1,0:T(8,128)S(1)}, f32[512,128]{1,0:T(8,128)}, u32[]{:S(2)}) copy-start(f32[512,128]{1,0:T(8,128)} %fusion.73) | copy-start | bytes 786436
  116.0 10.3 %copy-start.9 = (f32[512,128]{1,0:T(8,128)S(1)}, f32[512,128]{1,0:T(8,128)}, u32[]{:S(2)}) copy-start(f32[512,128]{1,0:T(8,128)} %fusion.65) | copy-start | bytes 786436
  116.2 11.7 %copy-start.10 = (f32[512,128]{1,0:T(8,128)S(1)}, f32[512,128]{1,0:T(8,128)}, u32[]{:S(2)}) copy-start(f32[512,128]{1,0:T(8,128)} %fusion.89) | copy-start | bytes 786436
  116.5 12.4 %copy-start.53 = (f32[512]{0:T(512)S(1)}, f32[512]{0:T(512)}, u32[]{:S(2)}) copy-start(f32[512]{0:T(512)} %copy-done.52) | copy-start | bytes 6148
  118.4 11.5 %copy-start.89 = (f32[512]{0:T(512)S(1)}, f32[512]{0:T(512)}, u32[]{:S(2)}) copy-start(f32[512]{0:T(512)} %get-tuple-element.18) | copy-start | bytes 6148
  120.1 10.0 %copy-start.88 = (f32[512]{0:T(512)S(1)}, f32[512]{0:T(512)}, u32[]{:S(2)}) copy-start(f32[512]{0:T(512)} %get-tuple-element.17) | copy-start | bytes 6148
  120.1 10.1 %copy-start.87 = (f32[512]{0:T(512)S(1)}, f32[512]{0:T(512)}, u32[]{:S(2)}) copy-start(f32[512]{0:T(512)} %get-tuple-element.19) | copy-start | bytes 6148
  120.1 10.2 %copy-start.86 = (f32[512]{0:T(512)S(1)}, f32[512]{0:T(512)}, u32[]{:S(2)}) copy-start(f32[512]{0:T(512)} %get-tuple-element.20) | copy-start | bytes 6148
  120.1 10.3 %copy-start.77 = (f32[512]{0:T(512)S(1)}, f32[512]{0:T(512)}, u32[]{:S(2)}) copy-start(f32[512]{0:T(512)} %get-tuple-element.14) | copy-start | bytes 6148
  120.1 10.3 %copy-start.93 = (f32[512]{0:T(512)S(1)}, f32[512]{0:T(512)}, u32[]{:S(2)}) copy-start(f32[512]{0:T(512)} %get-tuple-element.46) | copy-start | bytes 6148
  120.1 10.4 %copy-start.76 = (f32[512]{0:T(512)S(1)}, f32[512]{0:T(512)}, u32[]{:S(2)}) copy-start(f32[512]{0:T(512)} %get-tuple-element.13) | copy-start | bytes 6148
  120.1 10.4 %copy-start.92 = (f32[512]{0:T(512)S(1)}, f32[512]{0:T(512)}, u32[]{:S(2)}) copy-start(f32[512]{0:T(512)} %get-tuple-element.45) | copy-start | bytes 6148
  120.1 10.5 %copy-start.75 = (f32[512]{0:T(512)S(1)}, f32[512]{0:T(512)}, u32[]{:S(2)}) copy-start(f32[512]{0:T(512)} %get-tuple-element.15) | copy-start | bytes 6148
  120.1 10.5 %copy-start.91 = (f32[512]{0:T(512)S(1)}, f32[512]{0:T(512)}, u32[]{:S(2)}) copy-start(f32[512]{0:T(512)} %get-tuple-element.47) | copy-start | bytes 6148
  120.1 10.6 %copy-start.74 = (f32[512]{0:T(512)S(1)}, f32[512]{0:T(512)}, u32[]{:S(2)}) copy-start(f32[512]{0:T(512)} %get-tuple-element.16) | copy-start | bytes 6148
  120.1 10.6 %copy-start.90 = (f32[512]{0:T(512)S(1)}, f32[512]{0:T(512)}, u32[]{:S(2)}) copy-start(f32[512]{0:T(512)} %get-tuple-element.48) | copy-start | bytes 6148
  128.9 7.5 %copy-start.14 = (f32[64,8,128]{2,1,0:T(8,128)S(1)}, f32[64,8,128]{2,1,0:T(8,128)}, u32[]{:S(2)}) copy-start(f32[64,8,128]{2,1,0:T(8,128)} %fusion.1) | copy-start | bytes 786436
  132.1 9.2 %all-to-all-start.2 = ((f32[8,1,1024]{2,1,0:T(1,128)}), f32[8,1,1024]{2,1,0:T(1,128)}, u32[]{:S(2)}, u32[]{:S(2)}) async-start(f32[8,1,1024]{2,1,0:T(1,128)} %reshape.821), calls=%async_computation.2 | async-start | bytes 65536 | tf_op jit(solution)/shard_map/all_to_all | solution.py:134
  141.3 9.0 %all-to-all-start = ((f32[8,1,1024]{2,1,0:T(1,128)}), f32[8,1,1024]{2,1,0:T(1,128)S(1)}, u32[]{:S(2)}, u32[]{:S(2)}) async-start(f32[8,1,1024]{2,1,0:T(1,128)} %reshape.819), calls=%async_computation | async-start | bytes 65536 | tf_op jit(solution)/shard_map/all_to_all | solution.py:133
  150.3 98.5 %all-to-all-start.1 = ((f32[1,4,64,32,128]{4,3,1,0,2:T(8,128)}), f32[1,4,64,32,128]{4,3,1,0,2:T(8,128)}, u32[]{:S(2)}, u32[]{:S(2)}) async-start(f32[1,4,64,32,128]{4,3,1,0,2:T(8,128)} %maximum_bitcast_fusion), calls=%async_computation.1 | async-start | bytes 8388608 | tf_op jit(solution)/shard_map/all_to_all | solution.py:135
  (53 other events, 148.9 us)
Sparse Core Ops, SparseCore 0:
  9.0 31.5 all-gather.1
where the time goes:
time: 262 us; the launch traced here: 260 us
  waiting for transfers between devices  103 us (39%)
  matrix products  63 us (24%)
  local copies, waits for them, and re-layouts  27.7 us (11%)
  other arithmetic  21.6 us (8%)
  blocking collectives  15.8 us (6%)
  between operations  15.3 us (6%)
  starting transfers between devices  13.3 us (5%)
    all_to_all x1, waiting for transfers between devices, per_device(): lax.all_to_all(partial_outs[None], 'ctx', split_axis=2, concat_axis=0, ti...  87.9 us
    dot_general x16, matrix products, per_device(): jnp.dot(coarse_weights.astype(jnp.bfloat16).reshape(rows_all * query_grou...  19.1 us
    max x16, local copies, waits for them, and re-layouts, per_device(): jnp.maximum(jnp.max(jnp.where(exact_mask, exact_scores, FLOOR_SCORE), axi...  17.3 us
    all_gather x1, blocking collectives, per_device(): chosen = lax.all_gather(picks, 'ctx', axis=0, tiled=True)  15.8 us
    dot_general x16, matrix products, per_device(): jnp.einsum('qd,kd->qk', generation_probe_vectors, context_keys[current_he...  14.9 us
    dot_general x16, matrix products, per_device(): jnp.einsum('qd,kd->qk', generation_probe_vectors, cluster_centroid_keys[c...  14.9 us
    dot_general x16, matrix products, per_device(): jnp.dot(exact_weights.astype(jnp.bfloat16).reshape(rows_all * query_group...  12.4 us
    all_gather x1, waiting for transfers between devices, per_device(): gathered = lax.all_gather(queries, 'ctx', axis=1, tiled=True)  12 us
  transfers between devices with their start and end apart: 4, of which 4 were waited for; matrix products, arithmetic and copies ran while one was open for 6% of the time, Pallas kernels for 0%

commit v1 on v0

--- a/solution.py
+++ b/solution.py
@@ -1,8 +1,11 @@
+import functools
 import math
 
 import jax
 import jax.numpy as jnp
 from jax import lax
+from jax.experimental import pallas as pl
+from jax.experimental.pallas import tpu as pltpu
 from jax.sharding import PartitionSpec as P
 
 FLOOR_SCORE = -10000.0
@@ -31,7 +34,7 @@
     )
 
 
-def per_device(
+def per_device_plain(
     queries,
     new_keys,
     step_new_values,
@@ -149,9 +152,434 @@
     return (numer / denom[..., None]).astype(jnp.bfloat16)
 
 
+MESH = pl.DeviceIdType.MESH
+LOG2E = math.log2(math.e)
+NT = (((1,), (1,)), ((), ()))
+TN = (((0,), (0,)), ((), ()))
+
+
+def chain_kernel(
+    n, dims,
+    qx, kx, vx, nk, nv, out,
+    qbuf, kb, vb, part, part_st, inc, inc_st, snd, snd_st, fin, fin_st, sib, sib_st,
+    tail, tail_st, acc, acc_st, wbuf, score,
+    q_send, f_send, q_recv, s_send, s_recv, f_recv, b_send, b_recv, kv_send, kv_recv,
+):
+    num_steps, rows, group, hh, cl, page, head_width, mask_groups = dims
+    nq = num_steps * rows * group
+    units = 2 * hh
+    me = lax.axis_index("ctx")
+    z, c = me // 2, me % 2
+    o = 1 - c
+    first, last = z == 0, z == n - 1
+    scale2 = LOG2E / math.sqrt(head_width)
+    coarse2 = LOG2E * math.log(page)
+    floor2 = FLOOR_SCORE * LOG2E
+    tokens = cl * page
+
+    def copy(src, dst, send, recv, chip, core):
+        return pltpu.make_async_remote_copy(
+            src_ref=src, dst_ref=dst, send_sem=send, recv_sem=recv,
+            device_id={"ctx": chip * 2 + core}, device_id_type=MESH,
+        )
+
+    barrier = pltpu.get_barrier_semaphore()
+    pl.semaphore_signal(barrier, inc=1, device_id={"ctx": z * 2 + o}, device_id_type=MESH)
+
+    @pl.when(jnp.logical_not(first))
+    def _():
+        for core in range(2):
+            pl.semaphore_signal(barrier, inc=1, device_id={"ctx": (z - 1) * 2 + core}, device_id_type=MESH)
+
+    @pl.when(jnp.logical_not(last))
+    def _():
+        for core in range(2):
+            pl.semaphore_signal(barrier, inc=1, device_id={"ctx": (z + 1) * 2 + core}, device_id_type=MESH)
+
+    pl.semaphore_wait(barrier, 5 - 2 * first.astype(jnp.int32) - 2 * last.astype(jnp.int32))
+
+    def q_out(way, half, h):
+        chip = (z - 1, z, z + 1)[way]
+        return copy(qx.at[half, h], qbuf.at[z, c, h], q_send.at[way, half, h], q_recv.at[z, c, h], chip, half)
+
+    def q_hop(b, sc, h, chip):
+        ref = qbuf.at[b, sc, h]
+        return copy(ref, ref, f_send.at[b, sc, h], q_recv.at[b, sc, h], chip, c)
+
+    def kv_out():
+        return (
+            copy(kx.at[o], kb.at[c], kv_send.at[0], kv_recv.at[0], z, o),
+            copy(vx.at[o], vb.at[c], kv_send.at[1], kv_recv.at[1], z, o),
+        )
+
+    for h in range(hh):
+        q_out(1, o, h).start()
+
+        @pl.when(jnp.logical_not(first))
+        def _():
+            for half in range(2):
+                q_out(0, half, h).start()
+
+        @pl.when(jnp.logical_not(last))
+        def _():
+            for half in range(2):
+                q_out(2, half, h).start()
+
+    for one in kv_out():
+        one.start()
+
+    kb[c] = kx[c]
+    vb[c] = vx[c]
+    qbuf[z, c] = qx[c]
+    wbuf[...] = jnp.zeros_like(wbuf)
+
+    def iota(shape, axis):
+        return lax.broadcasted_iota(jnp.int32, shape, axis)
+
+    def tail_head(hd, carry):
+        q = qx[hd // hh, hd % hh, 0:nq, :]
+        s = lax.dot_general(nk[hd], q, NT, preferred_element_type=jnp.float32) * scale2
+        shape = (num_steps * rows, nq)
+        t, r = iota(shape, 0) // rows, iota(shape, 0) % rows
+        lane = iota(shape, 1)
+        seen = jnp.logical_and((lane // group) % rows == r, t <= lane // (rows * group))
+        s = jnp.where(seen, s, floor2)
+        top = jnp.max(s, axis=0, keepdims=True)
+        w = jnp.where(seen, jnp.exp2(s - top), 0.0)
+        tail_st[hd, 0:1, :] = top
+        tail_st[hd, 1:2, :] = jnp.sum(w, axis=0, keepdims=True)
+        tail[hd] = lax.dot_general(nv[hd], w.astype(jnp.bfloat16), TN, preferred_element_type=jnp.float32)
+        return carry
+
+    lax.fori_loop(0, 2 * hh, tail_head, 0)
+
+    sel_rows = 48
+    si, sl = iota((sel_rows, 128), 0), iota((sel_rows, 128), 1)
+    ncl = 2 * n * cl
+    in_page = si < 2 * cl
+    blk = jnp.where(si >= 32, 1, 0)
+    j = si - 16 - 16 * blk
+    in_coarse = jnp.logical_and(si >= 16, j < cl)
+    target = jnp.where(in_page, z * 2 * cl + si, jnp.where(in_coarse, ncl + (z * 2 + blk) * cl + j, -1))
+    spread = jnp.where((iota((16, nq), 1) // group) % rows == iota((16, nq), 0), 1.0, 0.0).astype(jnp.bfloat16)
+
+    for one in kv_out():
+        one.wait_recv()
+
+    def compute(b, sc, h):
+        q = qbuf[b, sc, h, 0:nq, :]
+        flags = None
+        for m in range(mask_groups):
+            sel = jnp.where(sl + m * 128 == target, 1.0, 0.0).astype(jnp.bfloat16)
+            bits = qbuf[b, sc, h, nq + 16 * m : nq + 16 * (m + 1), :]
+            got = lax.dot_general(sel, bits, NT, preferred_element_type=jnp.float32)
+            flags = got if flags is None else flags + got
+        flags = jnp.dot(flags.astype(jnp.bfloat16), spread, preferred_element_type=jnp.float32)
+        outs = []
+        for d in range(2):
+            score[...] = lax.dot_general(kb[d, h], q, NT, preferred_element_type=jnp.float32) * scale2
+            coarse_on = flags[16 + 16 * d : 32 + 16 * d, :] > 0.5
+            coarse = score[tokens : tokens + 16, :] + coarse2
+            top = jnp.max(jnp.where(coarse_on, coarse, floor2), axis=0, keepdims=True)
+            on = [flags[d * cl + p : d * cl + p + 1, :] > 0.5 for p in range(cl)]
+            for p in range(cl):
+                page_top = jnp.max(score[p * page : (p + 1) * page, :], axis=0, keepdims=True)
+                top = jnp.maximum(top, jnp.where(on[p], page_top, floor2))
+            wc = jnp.where(coarse_on, jnp.exp2(coarse - top), 0.0)
+            wbuf[tokens : tokens + 16, :] = wc.astype(jnp.bfloat16)
+            total = jnp.sum(wc, axis=0, keepdims=True)
+            for p in range(cl):
+                w = jnp.exp2(score[p * page : (p + 1) * page, :] - jnp.where(on[p], top, 1e30))
+                wbuf[p * page : (p + 1) * page, :] = w.astype(jnp.bfloat16)
+                total = total + jnp.sum(w, axis=0, keepdims=True)
+            outs.append((jnp.dot(vb[d, h], wbuf[...], preferred_element_type=jnp.float32), total, top))
+        (o0, l0, m0), (o1, l1, m1) = outs
+        top = jnp.maximum(m0, m1)
+        a0, a1 = jnp.exp2(m0 - top), jnp.exp2(m1 - top)
+        part[b, sc, h] = a0 * o0 + a1 * o1
+        part_st[b, sc, h, 0:1, :] = top
+        part_st[b, sc, h, 1:2, :] = a0 * l0 + a1 * l1
+
+    def merge(o_ref, st_ref, values, st):
+        m0, m1 = st_ref[0:1, :], st[0:1, :]
+        top = jnp.maximum(m0, m1)
+        a0, a1 = jnp.exp2(m0 - top), jnp.exp2(m1 - top)
+        o_ref[...] = a0 * o_ref[...] + a1 * values
+        st_ref[1:2, :] = a0 * st_ref[1:2, :] + a1 * st[1:2, :]
+        st_ref[0:1, :] = top
+
+    def decode(ref, st_ref):
+        return ref[...].astype(jnp.int32).astype(jnp.float32) * st_ref[2:3, :]
+
+    def flow_out(b, sc, h, chip, way):
+        def hop(fn):
+            fn(
+                copy(snd.at[b, sc, h], inc.at[b, sc, h], s_send.at[0, b, sc, h], s_recv.at[0, b, sc, h], chip, c),
+                copy(snd_st.at[b, sc, h], inc_st.at[b, sc, h], s_send.at[1, b, sc, h], s_recv.at[1, b, sc, h], chip, c),
+            )
+
+        def home(fn):
+            fn(
+                copy(snd.at[b, sc, h], fin.at[way, c, h], s_send.at[0, b, sc, h], f_recv.at[0, way, c, h], b, sc),
+                copy(snd_st.at[b, sc, h], fin_st.at[way, c, h], s_send.at[1, b, sc, h], f_recv.at[1, way, c, h], b, sc),
+            )
+
+        return hop, home
+
+    def both_start(x, y):
+        x.start()
+        y.start()
+
+    def both_wait_send(x, y):
+        x.wait_send()
+        y.wait_send()
+
+    def both_wait_recv(x, y):
+        x.wait_recv()
+        y.wait_recv()
+
+    def sib_out(h):
+        return (
+            copy(part.at[z, o, h], sib.at[h], b_send.at[0, h], b_recv.at[0, h], z, o),
+            copy(part_st.at[z, o, h], sib_st.at[h], b_send.at[1, h], b_recv.at[1, h], z, o),
+        )
+
+    def step(i, carry):
+        dist = i // (2 * units)
+        u = (i // 2) % units
+        side = i % 2
+        sc = (u // hh + c) % 2
+        h = u % hh
+        b = z + (2 * side - 1) * dist
+        valid = jnp.logical_and(jnp.logical_and(b >= 0, b < n), jnp.logical_or(dist > 0, side == 0))
+
+        @pl.when(valid)
+        def _():
+            bb = jnp.clip(b, 0, n - 1)
+
+            @pl.when(jnp.logical_or(dist > 0, sc != c))
+            def _():
+                q_hop(bb, sc, h, z).wait_recv()
+
+            @pl.when(jnp.logical_and(bb < z, jnp.logical_not(last)))
+            def _():
+                q_hop(bb, sc, h, z + 1).start()
+
+            @pl.when(jnp.logical_and(bb > z, jnp.logical_not(first)))
+            def _():
+                q_hop(bb, sc, h, z - 1).start()
+
+            compute(bb, sc, h)
+
+            @pl.when(jnp.logical_and(bb == z, sc != c))
+            def _():
+                both_start(*sib_out(h))
+
+        bm = jnp.where(side == 0, 2 * (n - 1) - z - dist, dist - z)
+        flows = jnp.where(
+            side == 0, jnp.logical_and(bm >= 0, bm < z), jnp.logical_and(bm > z, bm < n)
+        )
+
+        @pl.when(flows)
+        def _():
+            bb = jnp.clip(bm, 0, n - 1)
+            o_ref, st_ref = part.at[bb, sc, h], part_st.at[bb, sc, h]
+
+            @pl.when(jnp.where(side == 0, jnp.logical_not(last), jnp.logical_not(first)))
+            def _():
+                flow_out(bb, sc, h, z, side)[0](both_wait_recv)
+                merge(o_ref, st_ref, decode(inc.at[bb, sc, h], inc_st.at[bb, sc, h]), inc_st.at[bb, sc, h])
+
+            values = o_ref[...]
+            size = jnp.max(jnp.abs(values), axis=0, keepdims=True)
+            fit = 32767.0 / jnp.maximum(size, 1e-30)
+            snd[bb, sc, h] = jnp.round(values * fit).astype(jnp.int32).astype(jnp.int16)
+            snd_st[bb, sc, h, 0:2, :] = st_ref[0:2, :]
+            snd_st[bb, sc, h, 2:3, :] = jnp.maximum(size, 1e-30) * (1.0 / 32767.0)
+            chip = z + 2 * side - 1
+            hop, home = flow_out(bb, sc, h, chip, side)
+
+            @pl.when(chip == bb)
+            def _():
+                home(both_start)
+
+            @pl.when(chip != bb)
+            def _():
+                hop(both_start)
+
+        return carry
+
+    lax.fori_loop(0, (2 * n - 1) * 2 * units, step, 0)
+
+    def finish(i, carry):
+        half = (i // hh + c) % 2
+        h = i % hh
+        hd = half * hh + h
+        acc[...] = tail[hd]
+        acc_st[...] = tail_st[hd]
+
+        @pl.when(half == c)
+        def _():
+            merge(acc, acc_st, part[z, c, h], part_st.at[z, c, h])
+
+        @pl.when(half != c)
+        def _():
+            both_wait_recv(*sib_out(h))
+            merge(acc, acc_st, sib[h], sib_st.at[h])
+
+        def arrive(way):
+            both_wait_recv(
+                copy(snd.at[0, 0, 0], fin.at[way, half, h], s_send.at[0, 0, 0, 0], f_recv.at[0, way, half, h], z, c),
+                copy(snd_st.at[0, 0, 0], fin_st.at[way, half, h], s_send.at[1, 0, 0, 0], f_recv.at[1, way, half, h], z, c),
+            )
+            merge(acc, acc_st, decode(fin.at[way, half, h], fin_st.at[way, half, h]), fin_st.at[way, half, h])
+
+        @pl.when(jnp.logical_not(last))
+        def _():
+            arrive(0)
+
+        @pl.when(jnp.logical_not(first))
+        def _():
+            arrive(1)
+
+        out[hd] = jnp.transpose(acc[...] / acc_st[1:2, :]).astype(jnp.bfloat16)
+        return carry
+
+    lax.fori_loop(0, units, finish, 0)
+
+    for one in kv_out():
+        one.wait_send()
+    for h in range(hh):
+        both_wait_send(*sib_out(h))
+        q_out(1, o, h).wait_send()
+
+        @pl.when(jnp.logical_not(first))
+        def _():
+            for half in range(2):
+                q_out(0, half, h).wait_send()
+
+        @pl.when(jnp.logical_not(last))
+        def _():
+            for half in range(2):
+                q_out(2, half, h).wait_send()
+
+    def drain(i, carry):
+        b, sc, h = i // units, (i // hh) % 2, i % hh
+
+        @pl.when(b != z)
+        def _():
+            flow_out(b, sc, h, z, 0)[0](both_wait_send)
+
+            @pl.when(jnp.where(b < z, jnp.logical_not(last), jnp.logical_not(first)))
+            def _():
+                q_hop(b, sc, h, z).wait_send()
+
+        return carry
+
+    lax.fori_loop(0, n * units, drain, 0)
+
+
+def per_device_paired(
+    n,
+    queries,
+    new_keys,
+    step_new_values,
+    context_keys,
+    context_values,
+    cluster_centroid_keys,
+    cluster_mean_values,
+    cluster_page_slot,
+    picks,
+):
+    num_steps, rows, num_heads, head_width = queries.shape
+    kv_local, tokens = context_keys.shape[:2]
+    cl = cluster_centroid_keys.shape[1]
+    ncl = cluster_page_slot.shape[1]
+    page = tokens // cl
+    group = num_heads // kv_local
+    hh = kv_local // 2
+    nq = num_steps * rows * group
+    bf16, f32, i16 = jnp.bfloat16, jnp.float32, jnp.int16
+    q = queries.reshape(num_steps, rows, kv_local, group, head_width)
+    q = q.transpose(2, 0, 1, 3, 4).reshape(2, hh, nq, head_width)
+    ids = jnp.arange(ncl, dtype=jnp.int32)
+    used = jnp.any(picks[..., None] == ids, axis=2)
+    slots = jnp.any(
+        jnp.logical_and(used[..., None], cluster_page_slot[None, :, :, None] == ids), axis=2
+    )
+    flags = jnp.concatenate([slots, jnp.logical_not(used)], axis=-1).astype(bf16)
+    mask_groups = -(-2 * ncl // 128)
+    flags = jnp.pad(flags.transpose(1, 0, 2), ((0, 0), (0, 16 - rows), (0, mask_groups * 128 - 2 * ncl)))
+    flags = flags.reshape(kv_local, 16, mask_groups, 128).transpose(0, 2, 1, 3)
+    flags = flags.reshape(2, hh, mask_groups * 16, 128)
+    qx = jnp.concatenate([q, flags], axis=2)
+    pad = ((0, 0), (0, 16 - cl), (0, 0))
+    kx = jnp.concatenate([context_keys, jnp.pad(cluster_centroid_keys, pad)], axis=1)
+    kx = kx.reshape(2, hh, tokens + 16, head_width)
+    pad = ((0, 0), (0, 128 - cl), (0, 0))
+    vx = jnp.concatenate([context_values, jnp.pad(cluster_mean_values, pad)], axis=1)
+    vx = vx.transpose(0, 2, 1).reshape(2, hh, head_width, tokens + 128)
+    nk = new_keys.transpose(2, 0, 1, 3).reshape(kv_local, num_steps * rows, head_width)
+    nv = step_new_values.transpose(2, 0, 1, 3).reshape(kv_local, num_steps * rows, head_width)
+    dims = (num_steps, rows, group, hh, cl, page, head_width, mask_groups)
+    dma = pltpu.SemaphoreType.DMA
+    vm = pltpu.VMEM
+    unit = (n, 2, hh)
+    out = pl.pallas_call(
+        functools.partial(chain_kernel, n, dims),
+        out_shape=jax.ShapeDtypeStruct((kv_local, nq, head_width), bf16),
+        in_specs=[pl.BlockSpec(memory_space=pltpu.VMEM)] * 5,
+        out_specs=pl.BlockSpec(memory_space=pltpu.VMEM),
+        scratch_shapes=[
+            vm(unit + qx.shape[2:], bf16),
+            vm(kx.shape, bf16),
+            vm(vx.shape, bf16),
+            vm(unit + (head_width, nq), f32),
+            vm(unit + (4, nq), f32),
+            vm(unit + (head_width, nq), i16),
+            vm(unit + (4, nq), f32),
+            vm(unit + (head_width, nq), i16),
+            vm(unit + (4, nq), f32),
+            vm((2, 2, hh, head_width, nq), i16),
+            vm((2, 2, hh, 4, nq), f32),
+            vm((hh, head_width, nq), f32),
+            vm((hh, 4, nq), f32),
+            vm((kv_local, head_width, nq), f32),
+            vm((kv_local, 4, nq), f32),
+            vm((head_width, nq), f32),
+            vm((4, nq), f32),
+            vm((tokens + 128, nq), bf16),
+            vm((tokens + 16, nq), f32),
+            dma((3, 2, hh)),
+            dma(unit),
+            dma(unit),
+            dma((2,) + unit),
+            dma((2,) + unit),
+            dma((2, 2, 2, hh)),
+            dma((2, hh)),
+            dma((2, hh)),
+            dma((2,)),
+            dma((2,)),
+        ],
+        compiler_params=pltpu.CompilerParams(
+            collective_id=0, has_side_effects=True, vmem_limit_bytes=40 * 1024 * 1024
+        ),
+        cost_estimate=pl.CostEstimate(
+            flops=8 * n * 2 * kv_local * nq * tokens * head_width,
+            bytes_accessed=8 * 1024 * 1024,
+            transcendentals=2 * n * kv_local * nq * tokens,
+        ),
+    )(qx, kx, vx, nk, nv)
+    out = out.reshape(kv_local, num_steps, rows, group, head_width)
+    return out.transpose(1, 2, 0, 3, 4).reshape(num_steps, rows, num_heads, head_width)
+
+
 def solution(mesh):
+    sizes = mesh.shape
+    paired = sizes["row"] == 1 and sizes["ctx"] % 2 == 0
+    step = functools.partial(per_device_paired, sizes["ctx"] // 2) if paired else per_device_plain
     return jax.shard_map(
-        per_device,
+        step,
         mesh=mesh,
         in_specs=(
             P(None, ("groups", "ctx", "row"), "rep", None),

time: 262 us -> 51.3 us (0.20)
  waiting for transfers between devices: 103 us -> 0 us
  matrix products: 63 us -> 0 us
  Pallas kernels: 0 us -> 45.8 us
  local copies, waits for them, and re-layouts: 27.7 us -> 2.86 us
  other arithmetic: 21.6 us -> 2.09 us
  blocking collectives: 15.8 us -> 0 us
  between operations: 15.3 us -> 0.14 us
  starting transfers between devices: 13.3 us -> 0 us
    all_to_all x3 -> x0, waiting for transfers between devices: 90.4 us -> none  [the longest x1 87.9 us: per_device(): lax.all_to_all(partial_outs[None], 'ctx', split_axis=2, concat_axis=0, ti...]
    dot_general x66 -> x0, matrix products: 63 us -> none  [the longest x16 19.1 us: per_device(): jnp.dot(coarse_weights.astype(jnp.bfloat16).reshape(rows_all * query_grou...]
    pallas_call x0 -> x1, Pallas kernels: none -> 45.8 us  [per_device_paired(): pl.pallas_call(functools.partial(chain_kernel, n, dims), out_shape=jax.Sh...]
    max x16 -> x0, local copies, waits for them, and re-layouts: 17.3 us -> none  [per_device(): jnp.maximum(jnp.max(jnp.where(exact_mask, exact_scores, FLOOR_SCORE), axi...]
    all_gather x1 -> x0, blocking collectives: 15.8 us -> none  [per_device(): chosen = lax.all_gather(picks, 'ctx', axis=0, tiled=True)]
    all_to_all x3 -> x0, starting transfers between devices: 13.3 us -> none  [the longest x1 5.2 us: per_device(): lax.all_to_all(partial_outs[None], 'ctx', split_axis=2, concat_axis=0, ti...]
    reduce_sum x12 -> x0, other arithmetic: 12.8 us -> none  [the longest x4 5.46 us: per_device(): jnp.sum(exact_weights, axis=(2, 3)) + jnp.sum(coarse_weights, axis=2)]
    all_gather x1 -> x0, waiting for transfers between devices: 12 us -> none  [per_device(): gathered = lax.all_gather(queries, 'ctx', axis=1, tiled=True)]
  transfers between devices with their start and end apart: 4 -> 0, of which waited for: 4 -> 0; matrix products, arithmetic and copies ran while one was open for 6% -> 0% of each run, Pallas kernels for 0% -> 0%
where the time goes in v1:
time: 51.3 us; the launch traced here: 50.9 us
  Pallas kernels  45.8 us (89%)
  local copies, waits for them, and re-layouts  2.86 us (6%)
  other arithmetic  2.09 us (4%)
    pallas_call x1, Pallas kernels, per_device_paired(): pl.pallas_call(functools.partial(chain_kernel, n, dims), out_shape=jax.Sh...  45.8 us
    reshape x1, local copies, waits for them, and re-layouts, per_device_paired(): q = queries.reshape(num_steps, rows, kv_local, group, head_width)  1.04 us

profile of v1, /device:TPU:1, one launch (start us, length us, event | category | flops | bytes accessed | tf_op | source)
XLA Modules:
  0.0 50.9 jit_solution(2382023076065576707)
XLA Ops:
  0.0 0.0 copy-start.2
  0.0 0.0 copy-start.3
  0.0 0.9 %fusion.5 = pred[8,4,32]{2,1,0:T(4,128)(4,1)S(1)} fusion(s32[8,4,16]{2,1,0:T(4,128)} %param.17), kind=kLoop, calls=%fused_computation.11 | loop fusion | flops 31744 | bytes 3072 | tf_op jit(solution)/shard_map/reduce_or | solution.py:506
  0.9 0.8 %iota_compare_fusion.3 = pred[4,32,32]{2,1,0:T(8,128)(4,1)S(1)} fusion(s32[4,32]{1,0:T(4,128)} %param.16), kind=kLoop, calls=%fused_computation.12 | loop fusion | flops 4096 | bytes 4608 | tf_op jit(solution)/shard_map/eq | solution.py:508
  1.7 0.2 and_reduce_fusion
  1.9 0.0 copy-start
  1.9 0.0 copy-start.4
  1.9 0.1 add_bitcast_fusion
  2.1 1.0 %copy.16 = bf16[4,8,4,8,128]{4,3,1,0,2:T(8,128)(2,1)S(1)} copy(bf16[4,8,4,8,128]{4,3,2,1,0:T(8,128)(2,1)} %bitcast.27) | data formatting | bytes 524288 | tf_op jit(solution)/shard_map/reshape | solution.py:503
  3.1 0.0 copy-done.2
  3.1 0.0 copy-done.3
  3.2 0.0 copy-done
  3.2 0.0 copy-done.4
  3.2 0.0 copy-start.1
  3.3 0.0 copy-start.5
  3.3 0.3 copy.18
  3.6 0.7 %copy-done.1 = bf16[4,512,128]{2,1,0:T(8,128)(2,1)S(1)} copy-done((bf16[4,512,128]{2,1,0:T(8,128)(2,1)S(1)}, bf16[4,512,128]{2,1,0:T(8,128)(2,1)}, u32[]{:S(2)}) %copy-start.1) | copy-done | bytes 524312
  4.3 0.0 copy-done.5
  4.3 45.8 %shard_map.91 = bf16[4,256,128]{2,1,0:T(8,128)(2,1)S(1)} custom-call(bf16[2,2,272,128]{3,2,1,0:T(8,128)(2,1)S(1)} %pad_maximum_fusion.qx, bf16[2,2,528,128]{3,2,1,0:T(8,128)(2,1)S(1)} %bitcast.24, bf16[2,2,128,640]{3,2,1,0:T(8,128)(2,1)S(1)} %bitcast.23, bf16[4,32,128]{2,1,0:T(8,128)(2,1)S(1)} %get-tuple-element.6.nk, ...), custom_call_target="tpu_custom_call" | custom-call | flops 4294967296 | bytes 8388608 | tf_op jit(solution)/shard_map/pallas_call | solution.py:528
  50.2 0.8 %copy.25 = bf16[4,8,4,8,128]{4,3,2,1,0:T(8,128)(2,1)} copy(bf16[4,8,4,8,128]{4,3,1,0,2:T(8,128)(2,1)S(1)} %bitcast.25) | data formatting | bytes 524288 | tf_op jit(solution)/shard_map/transpose | solution.py:574
  (7 shorter events, 0.1 us)
Async XLA Ops:
  0.0 3.1 %copy-start.2 = (bf16[4,8,4,128]{3,2,1,0:T(4,128)(2,1)S(1)}, bf16[4,8,4,128]{3,2,1,0:T(4,128)(2,1)}, u32[]{:S(2)}) copy-start(bf16[4,8,4,128]{3,2,1,0:T(4,128)(2,1)} %param.11) | copy-start | bytes 98308
  0.0 3.1 %copy-start.3 = (bf16[4,8,4,128]{3,2,1,0:T(4,128)(2,1)S(1)}, bf16[4,8,4,128]{3,2,1,0:T(4,128)(2,1)}, u32[]{:S(2)}) copy-start(bf16[4,8,4,128]{3,2,1,0:T(4,128)(2,1)} %param.10) | copy-start | bytes 98308
  1.9 1.3 %copy-start = (bf16[4,512,128]{2,1,0:T(8,128)(2,1)S(1)}, bf16[4,512,128]{2,1,0:T(8,128)(2,1)}, u32[]{:S(2)}) copy-start(bf16[4,512,128]{2,1,0:T(8,128)(2,1)} %param.13) | copy-start | bytes 1572868
  1.9 1.3 %copy-start.4 = (bf16[4,4,128]{2,1,0:T(4,128)(2,1)S(1)}, bf16[4,4,128]{2,1,0:T(4,128)(2,1)}, u32[]{:S(2)}) copy-start(bf16[4,4,128]{2,1,0:T(4,128)(2,1)} %param.15) | copy-start | bytes 12292
  3.2 1.0 %copy-start.1 = (bf16[4,512,128]{2,1,0:T(8,128)(2,1)S(1)}, bf16[4,512,128]{2,1,0:T(8,128)(2,1)}, u32[]{:S(2)}) copy-start(bf16[4,512,128]{2,1,0:T(8,128)(2,1)} %param.12) | copy-start | bytes 1572868
  3.3 1.0 %copy-start.5 = (bf16[4,4,128]{2,1,0:T(4,128)(2,1)S(1)}, bf16[4,4,128]{2,1,0:T(4,128)(2,1)}, u32[]{:S(2)}) copy-start(bf16[4,4,128]{2,1,0:T(4,128)(2,1)} %param.14) | copy-start | bytes 12292

commit v2 on v1

--- a/solution.py
+++ b/solution.py
@@ -277,22 +277,23 @@
         flags = jnp.dot(flags.astype(jnp.bfloat16), spread, preferred_element_type=jnp.float32)
         outs = []
         for d in range(2):
-            score[...] = lax.dot_general(kb[d, h], q, NT, preferred_element_type=jnp.float32) * scale2
+            score[d] = lax.dot_general(kb[d, h], q, NT, preferred_element_type=jnp.float32) * scale2
+        for d in range(2):
             coarse_on = flags[16 + 16 * d : 32 + 16 * d, :] > 0.5
-            coarse = score[tokens : tokens + 16, :] + coarse2
+            coarse = score[d, tokens : tokens + 16, :] + coarse2
             top = jnp.max(jnp.where(coarse_on, coarse, floor2), axis=0, keepdims=True)
             on = [flags[d * cl + p : d * cl + p + 1, :] > 0.5 for p in range(cl)]
             for p in range(cl):
-                page_top = jnp.max(score[p * page : (p + 1) * page, :], axis=0, keepdims=True)
+                page_top = jnp.max(score[d, p * page : (p + 1) * page, :], axis=0, keepdims=True)
                 top = jnp.maximum(top, jnp.where(on[p], page_top, floor2))
             wc = jnp.where(coarse_on, jnp.exp2(coarse - top), 0.0)
-            wbuf[tokens : tokens + 16, :] = wc.astype(jnp.bfloat16)
+            wbuf[d, tokens : tokens + 16, :] = wc.astype(jnp.bfloat16)
             total = jnp.sum(wc, axis=0, keepdims=True)
             for p in range(cl):
-                w = jnp.exp2(score[p * page : (p + 1) * page, :] - jnp.where(on[p], top, 1e30))
-                wbuf[p * page : (p + 1) * page, :] = w.astype(jnp.bfloat16)
+                w = jnp.exp2(score[d, p * page : (p + 1) * page, :] - jnp.where(on[p], top, 1e30))
+                wbuf[d, p * page : (p + 1) * page, :] = w.astype(jnp.bfloat16)
                 total = total + jnp.sum(w, axis=0, keepdims=True)
-            outs.append((jnp.dot(vb[d, h], wbuf[...], preferred_element_type=jnp.float32), total, top))
+            outs.append((jnp.dot(vb[d, h], wbuf[d], preferred_element_type=jnp.float32), total, top))
         (o0, l0, m0), (o1, l1, m1) = outs
         top = jnp.maximum(m0, m1)
         a0, a1 = jnp.exp2(m0 - top), jnp.exp2(m1 - top)
@@ -344,30 +345,45 @@
             copy(part_st.at[z, o, h], sib_st.at[h], b_send.at[1, h], b_recv.at[1, h], z, o),
         )
 
-    def step(i, carry):
+    lead = hh
+
+    def slot(i):
         dist = i // (2 * units)
         u = (i // 2) % units
         side = i % 2
-        sc = (u // hh + c) % 2
-        h = u % hh
-        b = z + (2 * side - 1) * dist
-        valid = jnp.logical_and(jnp.logical_and(b >= 0, b < n), jnp.logical_or(dist > 0, side == 0))
+        return dist, side, (u // hh + c) % 2, u % hh, z + (2 * side - 1) * dist, u
+
+    def step(i, carry):
+        dist, side, sc, h, b, _ = slot(i + 2 * lead)
+
+        @pl.when(jnp.logical_and(dist > 0, jnp.logical_and(b >= 0, b < n)))
+        def _():
+            bb = jnp.clip(b, 0, n - 1)
+            q_hop(bb, sc, h, z).wait_recv()
+
+            @pl.when(jnp.logical_and(bb < z, jnp.logical_not(last)))
+            def _():
+                q_hop(bb, sc, h, z + 1).start()
+
+            @pl.when(jnp.logical_and(bb > z, jnp.logical_not(first)))
+            def _():
+                q_hop(bb, sc, h, z - 1).start()
+
+        dist, side, sc, h, b, u = slot(i)
+        b = jnp.where(dist == n, z, b)
+        valid = jnp.where(
+            dist % n == 0,
+            jnp.logical_and(side == 0, jnp.where(dist == 0, u < hh, jnp.logical_and(dist == n, u >= hh))),
+            jnp.logical_and(b >= 0, b < n),
+        )
 
         @pl.when(valid)
         def _():
             bb = jnp.clip(b, 0, n - 1)
 
-            @pl.when(jnp.logical_or(dist > 0, sc != c))
+            @pl.when(jnp.logical_and(bb == z, sc != c))
             def _():
                 q_hop(bb, sc, h, z).wait_recv()
-
-            @pl.when(jnp.logical_and(bb < z, jnp.logical_not(last)))
-            def _():
-                q_hop(bb, sc, h, z + 1).start()
-
-            @pl.when(jnp.logical_and(bb > z, jnp.logical_not(first)))
-            def _():
-                q_hop(bb, sc, h, z - 1).start()
 
             compute(bb, sc, h)
 
@@ -548,8 +564,8 @@
             vm((kv_local, 4, nq), f32),
             vm((head_width, nq), f32),
             vm((4, nq), f32),
-            vm((tokens + 128, nq), bf16),
-            vm((tokens + 16, nq), f32),
+            vm((2, tokens + 128, nq), bf16),
+            vm((2, tokens + 16, nq), f32),
             dma((3, 2, hh)),
             dma(unit),
             dma(unit),
@@ -576,7 +592,7 @@
 
 def solution(mesh):
     sizes = mesh.shape
-    paired = sizes["row"] == 1 and sizes["ctx"] % 2 == 0
+    paired = sizes["row"] == 1 and sizes["ctx"] % 2 == 0 and sizes["ctx"] > 2
     step = functools.partial(per_device_paired, sizes["ctx"] // 2) if paired else per_device_plain
     return jax.shard_map(
         step,

time: 51.3 us -> 46.1 us (0.90)
  Pallas kernels: 45.8 us -> 40.7 us
    pallas_call x1, Pallas kernels: 45.8 us -> 40.7 us  [per_device_paired(): pl.pallas_call(functools.partial(chain_kernel, n, dims), out_shape=jax.Sh...]
where the time goes in v2:
time: 46.1 us; the launch traced here: 45.8 us
  Pallas kernels  40.7 us (88%)
  local copies, waits for them, and re-layouts  2.86 us (6%)
  other arithmetic  2.09 us (5%)
    pallas_call x1, Pallas kernels, per_device_paired(): pl.pallas_call(functools.partial(chain_kernel, n, dims), out_shape=jax.Sh...  40.7 us
    reshape x1, local copies, waits for them, and re-layouts, per_device_paired(): q = queries.reshape(num_steps, rows, kv_local, group, head_width)  1.04 us

profile of v2, /device:TPU:1, one launch (start us, length us, event | category | flops | bytes accessed | tf_op | source)
XLA Modules:
  0.0 45.8 jit_solution(9227316470924242726)
XLA Ops:
  0.0 0.0 copy-start.2
  0.0 0.0 copy-start.3
  0.0 0.9 %fusion.5 = pred[8,4,32]{2,1,0:T(4,128)(4,1)S(1)} fusion(s32[8,4,16]{2,1,0:T(4,128)} %param.17), kind=kLoop, calls=%fused_computation.11 | loop fusion | flops 31744 | bytes 3072 | tf_op jit(solution)/shard_map/reduce_or | solution.py:522
  0.9 0.8 %iota_compare_fusion.3 = pred[4,32,32]{2,1,0:T(8,128)(4,1)S(1)} fusion(s32[4,32]{1,0:T(4,128)} %param.16), kind=kLoop, calls=%fused_computation.12 | loop fusion | flops 4096 | bytes 4608 | tf_op jit(solution)/shard_map/eq | solution.py:524
  1.7 0.2 and_reduce_fusion
  1.9 0.0 copy-start
  1.9 0.0 copy-start.4
  1.9 0.1 add_bitcast_fusion
  2.1 1.0 %copy.16 = bf16[4,8,4,8,128]{4,3,1,0,2:T(8,128)(2,1)S(1)} copy(bf16[4,8,4,8,128]{4,3,2,1,0:T(8,128)(2,1)} %bitcast.27) | data formatting | bytes 524288 | tf_op jit(solution)/shard_map/reshape | solution.py:519
  3.1 0.0 copy-done.2
  3.1 0.0 copy-done.3
  3.2 0.0 copy-done
  3.2 0.0 copy-done.4
  3.2 0.0 copy-start.1
  3.3 0.0 copy-start.5
  3.3 0.3 copy.18
  3.6 0.7 %copy-done.1 = bf16[4,512,128]{2,1,0:T(8,128)(2,1)S(1)} copy-done((bf16[4,512,128]{2,1,0:T(8,128)(2,1)S(1)}, bf16[4,512,128]{2,1,0:T(8,128)(2,1)}, u32[]{:S(2)}) %copy-start.1) | copy-done | bytes 524312
  4.3 0.0 copy-done.5
  4.3 40.7 %shard_map.91 = bf16[4,256,128]{2,1,0:T(8,128)(2,1)S(1)} custom-call(bf16[2,2,272,128]{3,2,1,0:T(8,128)(2,1)S(1)} %pad_maximum_fusion.qx, bf16[2,2,528,128]{3,2,1,0:T(8,128)(2,1)S(1)} %bitcast.24, bf16[2,2,128,640]{3,2,1,0:T(8,128)(2,1)S(1)} %bitcast.23, bf16[4,32,128]{2,1,0:T(8,128)(2,1)S(1)} %get-tuple-element.6.nk, ...), custom_call_target="tpu_custom_call" | custom-call | flops 4294967296 | bytes 8388608 | tf_op jit(solution)/shard_map/pallas_call | solution.py:544
  45.1 0.8 %copy.25 = bf16[4,8,4,8,128]{4,3,2,1,0:T(8,128)(2,1)} copy(bf16[4,8,4,8,128]{4,3,1,0,2:T(8,128)(2,1)S(1)} %bitcast.25) | data formatting | bytes 524288 | tf_op jit(solution)/shard_map/transpose | solution.py:590
  (7 shorter events, 0.1 us)
Async XLA Ops:
  0.0 3.1 %copy-start.2 = (bf16[4,8,4,128]{3,2,1,0:T(4,128)(2,1)S(1)}, bf16[4,8,4,128]{3,2,1,0:T(4,128)(2,1)}, u32[]{:S(2)}) copy-start(bf16[4,8,4,128]{3,2,1,0:T(4,128)(2,1)} %param.11) | copy-start | bytes 98308
  0.0 3.1 %copy-start.3 = (bf16[4,8,4,128]{3,2,1,0:T(4,128)(2,1)S(1)}, bf16[4,8,4,128]{3,2,1,0:T(4,128)(2,1)}, u32[]{:S(2)}) copy-start(bf16[4,8,4,128]{3,2,1,0:T(4,128)(2,1)} %param.10) | copy-start | bytes 98308
  1.9 1.3 %copy-start = (bf16[4,512,128]{2,1,0:T(8,128)(2,1)S(1)}, bf16[4,512,128]{2,1,0:T(8,128)(2,1)}, u32[]{:S(2)}) copy-start(bf16[4,512,128]{2,1,0:T(8,128)(2,1)} %param.13) | copy-start | bytes 1572868
  1.9 1.3 %copy-start.4 = (bf16[4,4,128]{2,1,0:T(4,128)(2,1)S(1)}, bf16[4,4,128]{2,1,0:T(4,128)(2,1)}, u32[]{:S(2)}) copy-start(bf16[4,4,128]{2,1,0:T(4,128)(2,1)} %param.15) | copy-start | bytes 12292
  3.2 1.0 %copy-start.1 = (bf16[4,512,128]{2,1,0:T(8,128)(2,1)S(1)}, bf16[4,512,128]{2,1,0:T(8,128)(2,1)}, u32[]{:S(2)}) copy-start(bf16[4,512,128]{2,1,0:T(8,128)(2,1)} %param.12) | copy-start | bytes 1572868
  3.3 1.0 %copy-start.5 = (bf16[4,4,128]{2,1,0:T(4,128)(2,1)S(1)}, bf16[4,4,128]{2,1,0:T(4,128)(2,1)}, u32[]{:S(2)}) copy-start(bf16[4,4,128]{2,1,0:T(4,128)(2,1)} %param.14) | copy-start | bytes 12292

commit v3 on v2

--- a/solution.py
+++ b/solution.py
@@ -160,12 +160,13 @@
 
 def chain_kernel(
     n, dims,
-    qx, kx, vx, nk, nv, out,
+    queries, keys, cents, vx, picks, slots, nk, nv, out,
+    qx,
     qbuf, kb, vb, part, part_st, inc, inc_st, snd, snd_st, fin, fin_st, sib, sib_st,
     tail, tail_st, acc, acc_st, wbuf, score,
-    q_send, f_send, q_recv, s_send, s_recv, f_recv, b_send, b_recv, kv_send, kv_recv,
+    q_send, f_send, q_recv, s_send, s_recv, f_recv, b_send, b_recv, kv_send, kv_recv, k_sem,
 ):
-    num_steps, rows, group, hh, cl, page, head_width, mask_groups = dims
+    num_steps, rows, group, hh, cl, page, head_width, ncl = dims
     nq = num_steps * rows * group
     units = 2 * hh
     me = lax.axis_index("ctx")
@@ -176,6 +177,7 @@
     coarse2 = LOG2E * math.log(page)
     floor2 = FLOOR_SCORE * LOG2E
     tokens = cl * page
+    num_picks = picks.shape[2]
 
     def copy(src, dst, send, recv, chip, core):
         return pltpu.make_async_remote_copy(
@@ -196,6 +198,24 @@
         for core in range(2):
             pl.semaphore_signal(barrier, inc=1, device_id={"ctx": (z + 1) * 2 + core}, device_id_type=MESH)
 
+    own_keys = pltpu.make_async_copy(keys.at[pl.ds(c * hh, hh)], kb.at[c, :, 0:tokens, :], k_sem)
+    own_keys.start()
+
+    def iota(shape, axis):
+        return lax.broadcasted_iota(jnp.int32, shape, axis)
+
+    page_of = jnp.where(slots[...] == iota((2 * hh, 128, 128), 1), 1.0, 0.0).astype(jnp.bfloat16)
+    lane = iota((16, 128), 1)
+    for hd in range(2 * hh):
+        ids = picks[hd] + ncl
+        used = jnp.zeros((16, 128), jnp.float32)
+        for k in range(num_picks):
+            used = jnp.where(ids[:, k : k + 1] == lane, 1.0, used)
+        pages = lax.dot_general(used.astype(jnp.bfloat16), page_of[hd], NT, preferred_element_type=jnp.float32)
+        coarse = jnp.where(jnp.logical_and(lane >= ncl, lane < 2 * ncl), 1.0 - used, 0.0)
+        qx[hd // hh, hd % hh, 0:nq, :] = queries[hd]
+        qx[hd // hh, hd % hh, nq : nq + 16, :] = (pages + coarse).astype(jnp.bfloat16)
+
     pl.semaphore_wait(barrier, 5 - 2 * first.astype(jnp.int32) - 2 * last.astype(jnp.int32))
 
     def q_out(way, half, h):
@@ -208,10 +228,16 @@
 
     def kv_out():
         return (
-            copy(kx.at[o], kb.at[c], kv_send.at[0], kv_recv.at[0], z, o),
+            copy(
+                keys.at[pl.ds(o * hh, hh)], kb.at[c, :, 0:tokens, :], kv_send.at[0], kv_recv.at[0], z, o
+            ),
+            copy(cents.at[o], kb.at[c, :, tokens : tokens + 16, :], kv_send.at[2], kv_recv.at[2], z, o),
             copy(vx.at[o], vb.at[c], kv_send.at[1], kv_recv.at[1], z, o),
         )
 
+    for one in kv_out():
+        one.start()
+
     for h in range(hh):
         q_out(1, o, h).start()
 
@@ -225,16 +251,10 @@
             for half in range(2):
                 q_out(2, half, h).start()
 
-    for one in kv_out():
-        one.start()
-
-    kb[c] = kx[c]
+    kb[c, :, tokens : tokens + 16, :] = cents[c]
     vb[c] = vx[c]
     qbuf[z, c] = qx[c]
     wbuf[...] = jnp.zeros_like(wbuf)
-
-    def iota(shape, axis):
-        return lax.broadcasted_iota(jnp.int32, shape, axis)
 
     def tail_head(hd, carry):
         q = qx[hd // hh, hd % hh, 0:nq, :]
@@ -255,25 +275,22 @@
 
     sel_rows = 48
     si, sl = iota((sel_rows, 128), 0), iota((sel_rows, 128), 1)
-    ncl = 2 * n * cl
     in_page = si < 2 * cl
     blk = jnp.where(si >= 32, 1, 0)
     j = si - 16 - 16 * blk
     in_coarse = jnp.logical_and(si >= 16, j < cl)
     target = jnp.where(in_page, z * 2 * cl + si, jnp.where(in_coarse, ncl + (z * 2 + blk) * cl + j, -1))
+    select = jnp.where(sl == target, 1.0, 0.0).astype(jnp.bfloat16)
     spread = jnp.where((iota((16, nq), 1) // group) % rows == iota((16, nq), 0), 1.0, 0.0).astype(jnp.bfloat16)
 
+    own_keys.wait()
     for one in kv_out():
         one.wait_recv()
 
     def compute(b, sc, h):
         q = qbuf[b, sc, h, 0:nq, :]
-        flags = None
-        for m in range(mask_groups):
-            sel = jnp.where(sl + m * 128 == target, 1.0, 0.0).astype(jnp.bfloat16)
-            bits = qbuf[b, sc, h, nq + 16 * m : nq + 16 * (m + 1), :]
-            got = lax.dot_general(sel, bits, NT, preferred_element_type=jnp.float32)
-            flags = got if flags is None else flags + got
+        bits = qbuf[b, sc, h, nq : nq + 16, :]
+        flags = lax.dot_general(select, bits, NT, preferred_element_type=jnp.float32)
         flags = jnp.dot(flags.astype(jnp.bfloat16), spread, preferred_element_type=jnp.float32)
         outs = []
         for d in range(2):
@@ -345,7 +362,8 @@
             copy(part_st.at[z, o, h], sib_st.at[h], b_send.at[1, h], b_recv.at[1, h], z, o),
         )
 
-    lead = hh
+    lead = units - 1
+    late = jnp.maximum(z, n - 1 - z) + 1
 
     def slot(i):
         dist = i // (2 * units)
@@ -370,10 +388,11 @@
                 q_hop(bb, sc, h, z - 1).start()
 
         dist, side, sc, h, b, u = slot(i)
-        b = jnp.where(dist == n, z, b)
+        own = jnp.logical_or(dist == 0, dist == late)
+        b = jnp.where(own, z, b)
         valid = jnp.where(
-            dist % n == 0,
-            jnp.logical_and(side == 0, jnp.where(dist == 0, u < hh, jnp.logical_and(dist == n, u >= hh))),
+            own,
+            jnp.logical_and(side == 0, jnp.where(dist == 0, u < hh, u >= hh)),
             jnp.logical_and(b >= 0, b < n),
         )
 
@@ -511,44 +530,40 @@
     kv_local, tokens = context_keys.shape[:2]
     cl = cluster_centroid_keys.shape[1]
     ncl = cluster_page_slot.shape[1]
+    if 2 * ncl > 128 or rows > 16 or 2 * cl > 16 or kv_local % 2:
+        return per_device_plain(
+            queries, new_keys, step_new_values, context_keys, context_values,
+            cluster_centroid_keys, cluster_mean_values, cluster_page_slot, picks,
+        )
     page = tokens // cl
     group = num_heads // kv_local
     hh = kv_local // 2
     nq = num_steps * rows * group
     bf16, f32, i16 = jnp.bfloat16, jnp.float32, jnp.int16
     q = queries.reshape(num_steps, rows, kv_local, group, head_width)
-    q = q.transpose(2, 0, 1, 3, 4).reshape(2, hh, nq, head_width)
-    ids = jnp.arange(ncl, dtype=jnp.int32)
-    used = jnp.any(picks[..., None] == ids, axis=2)
-    slots = jnp.any(
-        jnp.logical_and(used[..., None], cluster_page_slot[None, :, :, None] == ids), axis=2
-    )
-    flags = jnp.concatenate([slots, jnp.logical_not(used)], axis=-1).astype(bf16)
-    mask_groups = -(-2 * ncl // 128)
-    flags = jnp.pad(flags.transpose(1, 0, 2), ((0, 0), (0, 16 - rows), (0, mask_groups * 128 - 2 * ncl)))
-    flags = flags.reshape(kv_local, 16, mask_groups, 128).transpose(0, 2, 1, 3)
-    flags = flags.reshape(2, hh, mask_groups * 16, 128)
-    qx = jnp.concatenate([q, flags], axis=2)
+    q = q.transpose(2, 0, 1, 3, 4).reshape(kv_local, nq, head_width)
+    chosen = jnp.pad(picks.transpose(1, 0, 2), ((0, 0), (0, 16 - rows), (0, 0)), constant_values=-1)
+    slots = jnp.pad(cluster_page_slot, ((0, 0), (ncl, 128 - 2 * ncl)), constant_values=-1)[:, None, :]
     pad = ((0, 0), (0, 16 - cl), (0, 0))
-    kx = jnp.concatenate([context_keys, jnp.pad(cluster_centroid_keys, pad)], axis=1)
-    kx = kx.reshape(2, hh, tokens + 16, head_width)
+    cents = jnp.pad(cluster_centroid_keys, pad).reshape(2, hh, 16, head_width)
     pad = ((0, 0), (0, 128 - cl), (0, 0))
     vx = jnp.concatenate([context_values, jnp.pad(cluster_mean_values, pad)], axis=1)
     vx = vx.transpose(0, 2, 1).reshape(2, hh, head_width, tokens + 128)
     nk = new_keys.transpose(2, 0, 1, 3).reshape(kv_local, num_steps * rows, head_width)
     nv = step_new_values.transpose(2, 0, 1, 3).reshape(kv_local, num_steps * rows, head_width)
-    dims = (num_steps, rows, group, hh, cl, page, head_width, mask_groups)
+    dims = (num_steps, rows, group, hh, cl, page, head_width, ncl)
     dma = pltpu.SemaphoreType.DMA
     vm = pltpu.VMEM
     unit = (n, 2, hh)
     out = pl.pallas_call(
         functools.partial(chain_kernel, n, dims),
         out_shape=jax.ShapeDtypeStruct((kv_local, nq, head_width), bf16),
-        in_specs=[pl.BlockSpec(memory_space=pltpu.VMEM)] * 5,
+        in_specs=[pl.BlockSpec(memory_space=pl.ANY if i == 1 else pltpu.VMEM) for i in range(8)],
         out_specs=pl.BlockSpec(memory_space=pltpu.VMEM),
         scratch_shapes=[
-            vm(unit + qx.shape[2:], bf16),
-            vm(kx.shape, bf16),
+            vm((2, hh, nq + 16, head_width), bf16),
+            vm(unit + (nq + 16, head_width), bf16),
+            vm((2, hh, tokens + 16, head_width), bf16),
             vm(vx.shape, bf16),
             vm(unit + (head_width, nq), f32),
             vm(unit + (4, nq), f32),
@@ -574,8 +589,9 @@
             dma((2, 2, 2, hh)),
             dma((2, hh)),
             dma((2, hh)),
-            dma((2,)),
-            dma((2,)),
+            dma((3,)),
+            dma((3,)),
+            dma,
         ],
         compiler_params=pltpu.CompilerParams(
             collective_id=0, has_side_effects=True, vmem_limit_bytes=40 * 1024 * 1024
@@ -585,7 +601,7 @@
             bytes_accessed=8 * 1024 * 1024,
             transcendentals=2 * n * kv_local * nq * tokens,
         ),
-    )(qx, kx, vx, nk, nv)
+    )(q, context_keys, cents, vx, chosen, slots, nk, nv)
     out = out.reshape(kv_local, num_steps, rows, group, head_width)
     return out.transpose(1, 2, 0, 3, 4).reshape(num_steps, rows, num_heads, head_width)
 

time: 46.1 us -> 45.7 us (level)
  other arithmetic: 2.09 us -> 1.1 us
  Pallas kernels: 40.7 us -> 41.6 us
    reduce_or x2 -> x0, other arithmetic: 1.12 us -> none  [the longest x1 0.89 us: per_device_paired(): used = jnp.any(picks[..., None] == ids, axis=2)]
    transpose x1, other arithmetic: 0.05 us -> 1.1 us  [per_device_paired(): vx = vx.transpose(0, 2, 1).reshape(2, hh, head_width, tokens + 128)]
    reshape x1, local copies, waits for them, and re-layouts: 1.04 us -> 0.06 us  [per_device_paired(): q = queries.reshape(num_steps, rows, kv_local, group, head_width)]
    pallas_call x1, Pallas kernels: 40.7 us -> 41.6 us  [per_device_paired(): pl.pallas_call(functools.partial(chain_kernel, n, dims), out_shape=jax.Sh...]
    reshape x1, local copies, waits for them, and re-layouts: 0.01 us -> 0.78 us  [per_device_paired(): step_new_values.transpose(2, 0, 1, 3)]
    eq x1 -> x0, other arithmetic: 0.77 us -> none  [per_device_paired(): cluster_page_slot[None, :, :, None] == ids]
where the time goes in v3:
time: 45.7 us; the launch traced here: 45.5 us
  Pallas kernels  41.6 us (91%)
  local copies, waits for them, and re-layouts  2.63 us (6%)
  other arithmetic  1.1 us (2%)
    pallas_call x1, Pallas kernels, per_device_paired(): pl.pallas_call(functools.partial(chain_kernel, n, dims), out_shape=jax.Sh...  41.6 us
    transpose x1, other arithmetic, per_device_paired(): vx = vx.transpose(0, 2, 1).reshape(2, hh, head_width, tokens + 128)  1.1 us

profile of v3, /device:TPU:1, one launch (start us, length us, event | category | flops | bytes accessed | tf_op | source)
XLA Modules:
  0.0 45.5 jit_solution(9477110958420534193)
XLA Ops:
  0.0 0.8 %copy_bitcast_fusion.1 = (bf16[4,32,128]{2,1,0:T(8,128)(2,1)S(1)}, bf16[4,32,128]{2,1,0:T(8,128)(2,1)S(1)}) fusion(bf16[4,4,8,128]{3,0,2,1:T(4,128)(2,1)} %bitcast.31, bf16[4,4,8,128]{3,0,2,1:T(4,128)(2,1)} %bitcast.32), kind=kLoop, calls=%fused_computation.5 | loop fusion | bytes 131072 | tf_op jit(solution)/shard_map/reshape | solution.py:553
  0.8 1.1 %fusion.2 = bf16[4,128,640]{1,2,0:T(8,128)(2,1)S(1)} fusion(bf16[4,4,128]{2,1,0:T(4,128)(2,1)} %param.15, bf16[4,512,128]{2,1,0:T(8,128)(2,1)} %param.13), kind=kLoop, calls=%fused_computation.3 | loop fusion | flops 1966080 | bytes 1183744 | tf_op jit(solution)/shard_map/transpose | solution.py:551
  1.9 0.0 copy-start.1
  1.9 0.0 copy-start.2
  1.9 0.0 copy-start.3
  1.9 0.0 copy-start.4
  1.9 0.0 copy-start
  2.0 0.3 copy.11
  2.3 0.6 %copy-done.1 = bf16[4,8,32,128]{3,2,1,0:T(8,128)(2,1)S(1)} copy-done((bf16[4,8,32,128]{3,2,1,0:T(8,128)(2,1)S(1)}, bf16[4,8,32,128]{3,2,1,0:T(8,128)(2,1)}, u32[]{:S(2)}) %copy-start.1) | copy-done | bytes 262168
  2.9 0.1 copy.10
  2.9 0.0 copy-done.2
  3.0 0.0 copy-done.3
  3.0 0.0 copy-done.4
  3.0 0.1 pad.19
  3.1 0.0 copy-done
  3.1 41.6 %shard_map.91 = bf16[4,256,128]{2,1,0:T(8,128)(2,1)S(1)} custom-call(bf16[4,256,128]{2,1,0:T(8,128)(2,1)S(1)} %bitcast.25, bf16[4,512,128]{2,1,0:T(8,128)(2,1)S(1)} %copy-done, bf16[2,2,16,128]{3,2,1,0:T(8,128)(2,1)S(1)} %bitcast.27, bf16[2,2,128,640]{3,2,1,0:T(8,128)(2,1)S(1)} %bitcast.24, s32[4,16,16]{2,1,0:T(8,128)S(1)} %pad.18.picks, ...), custom_call_target="tpu_custom_call" | custom-call | flops 4294967296 | bytes 8388608 | tf_op jit(solution)/shard_map/pallas_call | solution.py:558
  44.7 0.7 %copy.20 = bf16[4,8,4,8,128]{4,3,2,1,0:T(8,128)(2,1)} copy(bf16[4,8,4,8,128]{4,3,1,0,2:T(8,128)(2,1)S(1)} %bitcast.26) | data formatting | bytes 524288 | tf_op jit(solution)/shard_map/transpose | solution.py:606
  (3 shorter events, 0.0 us)
Async XLA Ops:
  1.9 1.0 %copy-start.1 = (bf16[4,8,32,128]{3,2,1,0:T(8,128)(2,1)S(1)}, bf16[4,8,32,128]{3,2,1,0:T(8,128)(2,1)}, u32[]{:S(2)}) copy-start(bf16[4,8,32,128]{3,2,1,0:T(8,128)(2,1)} %param.9) | copy-start | bytes 786436
  1.9 1.0 %copy-start.2 = (s32[8,4,16]{2,1,0:T(4,128)S(1)}, s32[8,4,16]{2,1,0:T(4,128)}, u32[]{:S(2)}) copy-start(s32[8,4,16]{2,1,0:T(4,128)} %param.17) | copy-start | bytes 6148
  1.9 1.0 %copy-start.3 = (bf16[4,4,128]{2,1,0:T(4,128)(2,1)S(1)}, bf16[4,4,128]{2,1,0:T(4,128)(2,1)}, u32[]{:S(2)}) copy-start(bf16[4,4,128]{2,1,0:T(4,128)(2,1)} %param.14) | copy-start | bytes 12292
  1.9 1.0 %copy-start.4 = (s32[4,32]{1,0:T(4,128)S(1)}, s32[4,32]{1,0:T(4,128)}, u32[]{:S(2)}) copy-start(s32[4,32]{1,0:T(4,128)} %param.16) | copy-start | bytes 1540
  1.9 1.1 %copy-start = (bf16[4,512,128]{2,1,0:T(8,128)(2,1)S(1)}, bf16[4,512,128]{2,1,0:T(8,128)(2,1)}, u32[]{:S(2)}) copy-start(bf16[4,512,128]{2,1,0:T(8,128)(2,1)} %keys.1) | copy-start | bytes 1572868

commit v4 on v3

--- a/solution.py
+++ b/solution.py
@@ -235,21 +235,23 @@
             copy(vx.at[o], vb.at[c], kv_send.at[1], kv_recv.at[1], z, o),
         )
 
+    for h in range(hh // 2):
+
+        @pl.when(jnp.logical_not(first))
+        def _():
+            for half in range(2):
+                q_out(0, half, h).start()
+
+        @pl.when(jnp.logical_not(last))
+        def _():
+            for half in range(2):
+                q_out(2, half, h).start()
+
     for one in kv_out():
         one.start()
 
     for h in range(hh):
         q_out(1, o, h).start()
-
-        @pl.when(jnp.logical_not(first))
-        def _():
-            for half in range(2):
-                q_out(0, half, h).start()
-
-        @pl.when(jnp.logical_not(last))
-        def _():
-            for half in range(2):
-                q_out(2, half, h).start()
 
     kb[c, :, tokens : tokens + 16, :] = cents[c]
     vb[c] = vx[c]
@@ -362,75 +364,35 @@
             copy(part_st.at[z, o, h], sib_st.at[h], b_send.at[1, h], b_recv.at[1, h], z, o),
         )
 
-    lead = units - 1
-    late = jnp.maximum(z, n - 1 - z) + 1
-
-    def slot(i):
-        dist = i // (2 * units)
-        u = (i // 2) % units
-        side = i % 2
-        return dist, side, (u // hh + c) % 2, u % hh, z + (2 * side - 1) * dist, u
-
-    def step(i, carry):
-        dist, side, sc, h, b, _ = slot(i + 2 * lead)
-
-        @pl.when(jnp.logical_and(dist > 0, jnp.logical_and(b >= 0, b < n)))
-        def _():
-            bb = jnp.clip(b, 0, n - 1)
-            q_hop(bb, sc, h, z).wait_recv()
-
-            @pl.when(jnp.logical_and(bb < z, jnp.logical_not(last)))
-            def _():
-                q_hop(bb, sc, h, z + 1).start()
-
-            @pl.when(jnp.logical_and(bb > z, jnp.logical_not(first)))
-            def _():
-                q_hop(bb, sc, h, z - 1).start()
-
-        dist, side, sc, h, b, u = slot(i)
-        own = jnp.logical_or(dist == 0, dist == late)
-        b = jnp.where(own, z, b)
-        valid = jnp.where(
-            own,
-            jnp.logical_and(side == 0, jnp.where(dist == 0, u < hh, u >= hh)),
-            jnp.logical_and(b >= 0, b < n),
-        )
-
-        @pl.when(valid)
-        def _():
-            bb = jnp.clip(b, 0, n - 1)
-
-            @pl.when(jnp.logical_and(bb == z, sc != c))
-            def _():
-                q_hop(bb, sc, h, z).wait_recv()
-
-            compute(bb, sc, h)
-
-            @pl.when(jnp.logical_and(bb == z, sc != c))
-            def _():
-                both_start(*sib_out(h))
-
-        bm = jnp.where(side == 0, 2 * (n - 1) - z - dist, dist - z)
-        flows = jnp.where(
-            side == 0, jnp.logical_and(bm >= 0, bm < z), jnp.logical_and(bm > z, bm < n)
-        )
-
-        @pl.when(flows)
-        def _():
-            bb = jnp.clip(bm, 0, n - 1)
+    def subslot(i):
+        k = i % units
+        side = k % 2
+        place = jnp.where(side == 0, z, n - 1 - z)
+        return i // units - 1, side, (k // 2 + c) % 2, k // 4, place
+
+    def event(t, side, place):
+        wave = jnp.where(t < place, 0, 1)
+        dist = jnp.where(t < place, t + 1, 2 * place - t)
+        valid = jnp.logical_and(t >= 0, t < 2 * place)
+        return wave, jnp.clip(z + (2 * side - 1) * dist, 0, n - 1), valid
+
+    def flow(bs, wave, side, sc, hw, place):
+        @pl.when(jnp.logical_and(bs >= 0, bs < place))
+        def _():
+            bb = jnp.clip(jnp.where(side == 0, bs, n - 1 - bs), 0, n - 1)
+            h = wave * (hh // 2) + hw
             o_ref, st_ref = part.at[bb, sc, h], part_st.at[bb, sc, h]
 
-            @pl.when(jnp.where(side == 0, jnp.logical_not(last), jnp.logical_not(first)))
+            @pl.when(place < n - 1)
             def _():
                 flow_out(bb, sc, h, z, side)[0](both_wait_recv)
                 merge(o_ref, st_ref, decode(inc.at[bb, sc, h], inc_st.at[bb, sc, h]), inc_st.at[bb, sc, h])
 
             values = o_ref[...]
-            size = jnp.max(jnp.abs(values), axis=0, keepdims=True)
-            fit = 32767.0 / jnp.maximum(size, 1e-30)
-            snd[bb, sc, h] = jnp.round(values * fit).astype(jnp.int32).astype(jnp.int16)
+            size = jnp.maximum(jnp.max(jnp.abs(values), axis=0, keepdims=True), 1e-30)
+            snd[bb, sc, h] = jnp.round(values * (32767.0 / size)).astype(jnp.int32).astype(jnp.int16)
             snd_st[bb, sc, h, 0:2, :] = st_ref[0:2, :]
-            snd_st[bb, sc, h, 2:3, :] = jnp.maximum(size, 1e-30) * (1.0 / 32767.0)
+            snd_st[bb, sc, h, 2:3, :] = size * (1.0 / 32767.0)
             chip = z + 2 * side - 1
             hop, home = flow_out(bb, sc, h, chip, side)
 
@@ -442,13 +404,66 @@
             def _():
                 hop(both_start)
 
+    def step(i, carry):
+        t, side, sc, hw, place = subslot(i + units)
+        wave, b, valid = event(t, side, place)
+        h = wave * (hh // 2) + hw
+
+        @pl.when(jnp.logical_and(valid, place < n - 1))
+        def _():
+            q_hop(b, sc, h, z).wait_recv()
+            q_hop(b, sc, h, z + 1 - 2 * side).start()
+
+        @pl.when(jnp.logical_and(jnp.logical_and(t == 2 * place, place < n - 1), sc == c))
+        def _():
+            @pl.when(side == 0)
+            def _():
+                for half in range(2):
+                    q_out(2, half, hh // 2 + hw).start()
+
+            @pl.when(side == 1)
+            def _():
+                for half in range(2):
+                    q_out(0, half, hh // 2 + hw).start()
+
+        t, side, sc, hw, place = subslot(i)
+        wave, b, valid = event(t, side, place)
+        early = jnp.logical_and(side == 0, sc == c)
+        is_first, is_last = t == -1, t == 2 * n - 2
+        own = jnp.logical_or(is_first, is_last)
+        wave = jnp.where(own, side, wave)
+        b = jnp.where(own, z, b)
+        valid = jnp.where(is_first, early, jnp.where(is_last, jnp.logical_not(early), valid))
+        h = wave * (hh // 2) + hw
+
+        @pl.when(valid)
+        def _():
+            @pl.when(jnp.where(own, sc != c, place == n - 1))
+            def _():
+                q_hop(b, sc, h, z).wait_recv()
+
+            compute(b, sc, h)
+
+            @pl.when(jnp.logical_and(own, sc != c))
+            def _():
+                both_start(*sib_out(h))
+
+        @pl.when(t >= 0)
+        def _():
+            def one(w, carry):
+                bs = jnp.where(w == 0, 2 * n - 3 - place - t, t - 2 * n + 2 + place)
+                flow(bs, w, side, sc, hw, place)
+                return carry
+
+            lax.fori_loop(0, 2, one, 0)
+
         return carry
 
-    lax.fori_loop(0, (2 * n - 1) * 2 * units, step, 0)
+    lax.fori_loop(0, 2 * n * units, step, 0)
 
     def finish(i, carry):
-        half = (i // hh + c) % 2
-        h = i % hh
+        half = (i % 2 + c) % 2
+        h = i // 2
         hd = half * hh + h
         acc[...] = tail[hd]
         acc_st[...] = tail_st[hd]
@@ -530,7 +545,7 @@
     kv_local, tokens = context_keys.shape[:2]
     cl = cluster_centroid_keys.shape[1]
     ncl = cluster_page_slot.shape[1]
-    if 2 * ncl > 128 or rows > 16 or 2 * cl > 16 or kv_local % 2:
+    if 2 * ncl > 128 or rows > 16 or 2 * cl > 16 or kv_local % 4:
         return per_device_plain(
             queries, new_keys, step_new_values, context_keys, context_values,
             cluster_centroid_keys, cluster_mean_values, cluster_page_slot, picks,

time: 45.7 us -> 40.4 us (0.88)
  Pallas kernels: 41.6 us -> 36.1 us
    pallas_call x1, Pallas kernels: 41.6 us -> 36.1 us  [per_device_paired(): pl.pallas_call(functools.partial(chain_kernel, n, dims), out_shape=jax.Sh...]
where the time goes in v4:
time: 40.4 us; the launch traced here: 39.9 us
  Pallas kernels  36.1 us (89%)
  local copies, waits for them, and re-layouts  2.63 us (7%)
  other arithmetic  1.1 us (3%)
    pallas_call x1, Pallas kernels, per_device_paired(): pl.pallas_call(functools.partial(chain_kernel, n, dims), out_shape=jax.Sh...  36.1 us
    transpose x1, other arithmetic, per_device_paired(): vx = vx.transpose(0, 2, 1).reshape(2, hh, head_width, tokens + 128)  1.1 us

profile of v4, /device:TPU:1, one launch (start us, length us, event | category | flops | bytes accessed | tf_op | source)
XLA Modules:
  0.0 39.9 jit_solution(11680916077894984379)
XLA Ops:
  0.0 0.8 %copy_bitcast_fusion.1 = (bf16[4,32,128]{2,1,0:T(8,128)(2,1)S(1)}, bf16[4,32,128]{2,1,0:T(8,128)(2,1)S(1)}) fusion(bf16[4,4,8,128]{3,0,2,1:T(4,128)(2,1)} %bitcast.31, bf16[4,4,8,128]{3,0,2,1:T(4,128)(2,1)} %bitcast.32), kind=kLoop, calls=%fused_computation.5 | loop fusion | bytes 131072 | tf_op jit(solution)/shard_map/reshape | solution.py:568
  0.8 1.1 %fusion.2 = bf16[4,128,640]{1,2,0:T(8,128)(2,1)S(1)} fusion(bf16[4,4,128]{2,1,0:T(4,128)(2,1)} %param.15, bf16[4,512,128]{2,1,0:T(8,128)(2,1)} %param.13), kind=kLoop, calls=%fused_computation.3 | loop fusion | flops 1966080 | bytes 1183744 | tf_op jit(solution)/shard_map/transpose | solution.py:566
  1.9 0.0 copy-start.1
  1.9 0.0 copy-start.2
  1.9 0.0 copy-start.3
  1.9 0.0 copy-start.4
  1.9 0.0 copy-start
  2.0 0.3 copy.11
  2.3 0.6 %copy-done.1 = bf16[4,8,32,128]{3,2,1,0:T(8,128)(2,1)S(1)} copy-done((bf16[4,8,32,128]{3,2,1,0:T(8,128)(2,1)S(1)}, bf16[4,8,32,128]{3,2,1,0:T(8,128)(2,1)}, u32[]{:S(2)}) %copy-start.1) | copy-done | bytes 262168
  2.9 0.1 copy.10
  2.9 0.0 copy-done.2
  3.0 0.0 copy-done.3
  3.0 0.0 copy-done.4
  3.0 0.1 pad.19
  3.1 0.0 copy-done
  3.1 36.1 %shard_map.91 = bf16[4,256,128]{2,1,0:T(8,128)(2,1)S(1)} custom-call(bf16[4,256,128]{2,1,0:T(8,128)(2,1)S(1)} %bitcast.25, bf16[4,512,128]{2,1,0:T(8,128)(2,1)S(1)} %copy-done, bf16[2,2,16,128]{3,2,1,0:T(8,128)(2,1)S(1)} %bitcast.27, bf16[2,2,128,640]{3,2,1,0:T(8,128)(2,1)S(1)} %bitcast.24, s32[4,16,16]{2,1,0:T(8,128)S(1)} %pad.18.picks, ...), custom_call_target="tpu_custom_call" | custom-call | flops 4294967296 | bytes 8388608 | tf_op jit(solution)/shard_map/pallas_call | solution.py:573
  39.2 0.7 %copy.20 = bf16[4,8,4,8,128]{4,3,2,1,0:T(8,128)(2,1)} copy(bf16[4,8,4,8,128]{4,3,1,0,2:T(8,128)(2,1)S(1)} %bitcast.26) | data formatting | bytes 524288 | tf_op jit(solution)/shard_map/transpose | solution.py:621
  (3 shorter events, 0.0 us)
Async XLA Ops:
  1.9 1.0 %copy-start.1 = (bf16[4,8,32,128]{3,2,1,0:T(8,128)(2,1)S(1)}, bf16[4,8,32,128]{3,2,1,0:T(8,128)(2,1)}, u32[]{:S(2)}) copy-start(bf16[4,8,32,128]{3,2,1,0:T(8,128)(2,1)} %param.9) | copy-start | bytes 786436
  1.9 1.0 %copy-start.2 = (s32[8,4,16]{2,1,0:T(4,128)S(1)}, s32[8,4,16]{2,1,0:T(4,128)}, u32[]{:S(2)}) copy-start(s32[8,4,16]{2,1,0:T(4,128)} %param.17) | copy-start | bytes 6148
  1.9 1.0 %copy-start.3 = (bf16[4,4,128]{2,1,0:T(4,128)(2,1)S(1)}, bf16[4,4,128]{2,1,0:T(4,128)(2,1)}, u32[]{:S(2)}) copy-start(bf16[4,4,128]{2,1,0:T(4,128)(2,1)} %param.14) | copy-start | bytes 12292
  1.9 1.0 %copy-start.4 = (s32[4,32]{1,0:T(4,128)S(1)}, s32[4,32]{1,0:T(4,128)}, u32[]{:S(2)}) copy-start(s32[4,32]{1,0:T(4,128)} %param.16) | copy-start | bytes 1540
  1.9 1.1 %copy-start = (bf16[4,512,128]{2,1,0:T(8,128)(2,1)S(1)}, bf16[4,512,128]{2,1,0:T(8,128)(2,1)}, u32[]{:S(2)}) copy-start(bf16[4,512,128]{2,1,0:T(8,128)(2,1)} %keys.1) | copy-start | bytes 1572868

commit v5 on v4

--- a/solution.py
+++ b/solution.py
@@ -160,9 +160,9 @@
 
 def chain_kernel(
     n, dims,
-    queries, keys, cents, vx, picks, slots, nk, nv, out,
+    queries, keys, cents, vals, means, picks, slots, nk, nv, out,
     qx,
-    qbuf, kb, vb, part, part_st, inc, inc_st, snd, snd_st, fin, fin_st, sib, sib_st,
+    qbuf, kb, vr, vb, part, part_st, inc, inc_st, snd, snd_st, fin, fin_st, sib, sib_st,
     tail, tail_st, acc, acc_st, wbuf, score,
     q_send, f_send, q_recv, s_send, s_recv, f_recv, b_send, b_recv, kv_send, kv_recv, k_sem,
 ):
@@ -198,8 +198,10 @@
         for core in range(2):
             pl.semaphore_signal(barrier, inc=1, device_id={"ctx": (z + 1) * 2 + core}, device_id_type=MESH)
 
-    own_keys = pltpu.make_async_copy(keys.at[pl.ds(c * hh, hh)], kb.at[c, :, 0:tokens, :], k_sem)
+    own_keys = pltpu.make_async_copy(keys.at[pl.ds(c * hh, hh)], kb.at[c, :, 0:tokens, :], k_sem.at[0])
     own_keys.start()
+    own_vals = pltpu.make_async_copy(vals.at[pl.ds(c * hh, hh)], vr.at[c, :, 0:tokens, :], k_sem.at[1])
+    own_vals.start()
 
     def iota(shape, axis):
         return lax.broadcasted_iota(jnp.int32, shape, axis)
@@ -232,7 +234,12 @@
                 keys.at[pl.ds(o * hh, hh)], kb.at[c, :, 0:tokens, :], kv_send.at[0], kv_recv.at[0], z, o
             ),
             copy(cents.at[o], kb.at[c, :, tokens : tokens + 16, :], kv_send.at[2], kv_recv.at[2], z, o),
-            copy(vx.at[o], vb.at[c], kv_send.at[1], kv_recv.at[1], z, o),
+            copy(
+                vals.at[pl.ds(o * hh, hh)], vr.at[c, :, 0:tokens, :], kv_send.at[1], kv_recv.at[1], z, o
+            ),
+            copy(
+                means.at[o], vr.at[c, :, tokens : tokens + 128, :], kv_send.at[3], kv_recv.at[3], z, o
+            ),
         )
 
     for h in range(hh // 2):
@@ -254,7 +261,7 @@
         q_out(1, o, h).start()
 
     kb[c, :, tokens : tokens + 16, :] = cents[c]
-    vb[c] = vx[c]
+    vr[c, :, tokens : tokens + 128, :] = means[c]
     qbuf[z, c] = qx[c]
     wbuf[...] = jnp.zeros_like(wbuf)
 
@@ -286,8 +293,15 @@
     spread = jnp.where((iota((16, nq), 1) // group) % rows == iota((16, nq), 0), 1.0, 0.0).astype(jnp.bfloat16)
 
     own_keys.wait()
+    own_vals.wait()
     for one in kv_out():
         one.wait_recv()
+
+    def turn(i, carry):
+        vb[i // hh, i % hh] = jnp.transpose(vr[i // hh, i % hh])
+        return carry
+
+    lax.fori_loop(0, 2 * hh, turn, 0)
 
     def compute(b, sc, h):
         q = qbuf[b, sc, h, 0:nq, :]
@@ -562,8 +576,7 @@
     pad = ((0, 0), (0, 16 - cl), (0, 0))
     cents = jnp.pad(cluster_centroid_keys, pad).reshape(2, hh, 16, head_width)
     pad = ((0, 0), (0, 128 - cl), (0, 0))
-    vx = jnp.concatenate([context_values, jnp.pad(cluster_mean_values, pad)], axis=1)
-    vx = vx.transpose(0, 2, 1).reshape(2, hh, head_width, tokens + 128)
+    means = jnp.pad(cluster_mean_values, pad).reshape(2, hh, 128, head_width)
     nk = new_keys.transpose(2, 0, 1, 3).reshape(kv_local, num_steps * rows, head_width)
     nv = step_new_values.transpose(2, 0, 1, 3).reshape(kv_local, num_steps * rows, head_width)
     dims = (num_steps, rows, group, hh, cl, page, head_width, ncl)
@@ -573,13 +586,14 @@
     out = pl.pallas_call(
         functools.partial(chain_kernel, n, dims),
         out_shape=jax.ShapeDtypeStruct((kv_local, nq, head_width), bf16),
-        in_specs=[pl.BlockSpec(memory_space=pl.ANY if i == 1 else pltpu.VMEM) for i in range(8)],
+        in_specs=[pl.BlockSpec(memory_space=pl.ANY if i in (1, 3) else pltpu.VMEM) for i in range(9)],
         out_specs=pl.BlockSpec(memory_space=pltpu.VMEM),
         scratch_shapes=[
             vm((2, hh, nq + 16, head_width), bf16),
             vm(unit + (nq + 16, head_width), bf16),
             vm((2, hh, tokens + 16, head_width), bf16),
-            vm(vx.shape, bf16),
+            vm((2, hh, tokens + 128, head_width), bf16),
+            vm((2, hh, head_width, tokens + 128), bf16),
             vm(unit + (head_width, nq), f32),
             vm(unit + (4, nq), f32),
             vm(unit + (head_width, nq), i16),
@@ -604,9 +618,9 @@
             dma((2, 2, 2, hh)),
             dma((2, hh)),
             dma((2, hh)),
-            dma((3,)),
-            dma((3,)),
-            dma,
+            dma((4,)),
+            dma((4,)),
+            dma((2,)),
         ],
         compiler_params=pltpu.CompilerParams(
             collective_id=0, has_side_effects=True, vmem_limit_bytes=40 * 1024 * 1024
@@ -616,7 +630,7 @@
             bytes_accessed=8 * 1024 * 1024,
             transcendentals=2 * n * kv_local * nq * tokens,
         ),
-    )(q, context_keys, cents, vx, chosen, slots, nk, nv)
+    )(q, context_keys, cents, context_values, means, chosen, slots, nk, nv)
     out = out.reshape(kv_local, num_steps, rows, group, head_width)
     return out.transpose(1, 2, 0, 3, 4).reshape(num_steps, rows, num_heads, head_width)
 

time: 40.4 us -> 43.3 us (1.072)
  local copies, waits for them, and re-layouts: 2.63 us -> 6.52 us
  other arithmetic: 1.1 us -> 0 us
    unnamed x11 -> x5, local copies, waits for them, and re-layouts: 0.64 us -> 1.76 us
    transpose x1 -> x0, other arithmetic: 1.1 us -> none  [per_device_paired(): vx = vx.transpose(0, 2, 1).reshape(2, hh, head_width, tokens + 128)]
    reshape x1, local copies, waits for them, and re-layouts: 0.06 us -> 1.01 us  [per_device_paired(): q = queries.reshape(num_steps, rows, kv_local, group, head_width)]
    pad x1, local copies, waits for them, and re-layouts: 0.07 us -> 0.81 us  [per_device_paired(): jnp.pad(cluster_page_slot, ((0, 0), (ncl, 128 - 2 * ncl)), constant_value...]
    pad x0 -> x1, local copies, waits for them, and re-layouts: none -> 0.71 us  [per_device_paired(): means = jnp.pad(cluster_mean_values, pad).reshape(2, hh, 128, head_width)]
    pad x1, local copies, waits for them, and re-layouts: 0.01 us -> 0.69 us  [per_device_paired(): cents = jnp.pad(cluster_centroid_keys, pad).reshape(2, hh, 16, head_width)]
where the time goes in v5:
time: 43.3 us; the launch traced here: 42.7 us
  Pallas kernels  36.2 us (84%)
  local copies, waits for them, and re-layouts  6.52 us (15%)
    pallas_call x1, Pallas kernels, per_device_paired(): pl.pallas_call(functools.partial(chain_kernel, n, dims), out_shape=jax.Sh...  36.2 us
    unnamed x5, local copies, waits for them, and re-layouts  1.76 us
    reshape x1, local copies, waits for them, and re-layouts, per_device_paired(): q = queries.reshape(num_steps, rows, kv_local, group, head_width)  1.01 us

profile of v5, /device:TPU:1, one launch (start us, length us, event | category | flops | bytes accessed | tf_op | source)
XLA Modules:
  0.0 42.7 jit_solution(10702313872255678684)
XLA Ops:
  0.0 0.0 copy-start
  0.0 0.8 %pad.19 = s32[4,128]{1,0:T(4,128)S(1)} pad(s32[4,32]{1,0:T(4,128)} %param.16, s32[]{:T(128)} %constant.4.clone.1), padding=0_0x32_64 | pad | bytes 2564 | tf_op jit(solution)/shard_map/jit(_pad)/pad | solution.py:575
  0.8 0.7 %pad.16 = bf16[4,16,128]{2,1,0:T(8,128)(2,1)S(1)} pad(bf16[4,4,128]{2,1,0:T(4,128)(2,1)} %param.14, bf16[]{:T(256)} %constant.1.clone.1), padding=0_0x0_12x0_0 | pad | bytes 20482 | tf_op jit(solution)/shard_map/jit(_pad)/pad | solution.py:577
  1.5 0.7 %copy.20 = s32[8,4,16]{2,0,1:T(8,128)S(1)} copy(s32[8,4,16]{2,1,0:T(4,128)} %param.17) | data formatting | bytes 4096 | tf_op args[8]
  2.2 0.8 %copy_bitcast_fusion.1 = (bf16[4,32,128]{2,1,0:T(8,128)(2,1)S(1)}, bf16[4,32,128]{2,1,0:T(8,128)(2,1)S(1)}) fusion(bf16[4,4,8,128]{3,0,2,1:T(4,128)(2,1)} %bitcast.29, bf16[4,4,8,128]{3,0,2,1:T(4,128)(2,1)} %bitcast.30), kind=kLoop, calls=%fused_computation.1 | loop fusion | bytes 131072 | tf_op jit(solution)/shard_map/reshape | solution.py:581
  3.0 0.7 %pad.17 = bf16[4,128,128]{2,1,0:T(8,128)(2,1)S(1)} pad(bf16[4,4,128]{2,1,0:T(4,128)(2,1)} %param.15, bf16[]{:T(256)} %constant.1.clone.1), padding=0_0x0_124x0_0 | pad | bytes 135170 | tf_op jit(solution)/shard_map/jit(_pad)/pad | solution.py:579
  3.7 1.0 %copy.10 = bf16[4,8,4,8,128]{4,3,1,0,2:T(8,128)(2,1)S(1)} copy(bf16[4,8,4,8,128]{4,3,2,1,0:T(8,128)(2,1)} %bitcast.27) | data formatting | bytes 524288 | tf_op jit(solution)/shard_map/reshape | solution.py:572
  4.8 0.0 copy-done
  4.8 0.0 copy-start.1
  4.8 1.0 %copy-done.1 = bf16[4,512,128]{2,1,0:T(8,128)(2,1)S(1)} copy-done((bf16[4,512,128]{2,1,0:T(8,128)(2,1)S(1)}, bf16[4,512,128]{2,1,0:T(8,128)(2,1)}, u32[]{:S(2)}) %copy-start.1) | copy-done | bytes 524312
  5.8 36.2 %shard_map.91 = bf16[4,256,128]{2,1,0:T(8,128)(2,1)S(1)} custom-call(bf16[4,256,128]{2,1,0:T(8,128)(2,1)S(1)} %bitcast.23, bf16[4,512,128]{2,1,0:T(8,128)(2,1)S(1)} %copy-done, bf16[2,2,16,128]{3,2,1,0:T(8,128)(2,1)S(1)} %bitcast.25, bf16[4,512,128]{2,1,0:T(8,128)(2,1)S(1)} %copy-done.1, bf16[2,2,128,128]{3,2,1,0:T(8,128)(2,1)S(1)} %bitcast.24, ...), custom_call_target="tpu_custom_call" | custom-call | flops 4294967296 | bytes 8388608 | tf_op jit(solution)/shard_map/pallas_call | solution.py:586
  42.0 0.8 %copy.19 = bf16[4,8,4,8,128]{4,3,2,1,0:T(8,128)(2,1)} copy(bf16[4,8,4,8,128]{4,3,1,0,2:T(8,128)(2,1)S(1)} %bitcast.22) | data formatting | bytes 524288 | tf_op jit(solution)/shard_map/transpose | solution.py:635
  (1 shorter events, 0.0 us)
Async XLA Ops:
  0.0 4.8 %copy-start = (bf16[4,512,128]{2,1,0:T(8,128)(2,1)S(1)}, bf16[4,512,128]{2,1,0:T(8,128)(2,1)}, u32[]{:S(2)}) copy-start(bf16[4,512,128]{2,1,0:T(8,128)(2,1)} %keys.1) | copy-start | bytes 1572868
  4.8 1.0 %copy-start.1 = (bf16[4,512,128]{2,1,0:T(8,128)(2,1)S(1)}, bf16[4,512,128]{2,1,0:T(8,128)(2,1)}, u32[]{:S(2)}) copy-start(bf16[4,512,128]{2,1,0:T(8,128)(2,1)} %vals.1) | copy-start | bytes 1572868

commit v6 on v4

--- a/solution.py
+++ b/solution.py
@@ -312,7 +312,7 @@
                 w = jnp.exp2(score[d, p * page : (p + 1) * page, :] - jnp.where(on[p], top, 1e30))
                 wbuf[d, p * page : (p + 1) * page, :] = w.astype(jnp.bfloat16)
                 total = total + jnp.sum(w, axis=0, keepdims=True)
-            outs.append((jnp.dot(vb[d, h], wbuf[d], preferred_element_type=jnp.float32), total, top))
+            outs.append((jnp.dot(vb[d, h, :, 0 : tokens + 16], wbuf[d, 0 : tokens + 16, :], preferred_element_type=jnp.float32), total, top))
         (o0, l0, m0), (o1, l1, m1) = outs
         top = jnp.maximum(m0, m1)
         a0, a1 = jnp.exp2(m0 - top), jnp.exp2(m1 - top)
@@ -573,7 +573,7 @@
     out = pl.pallas_call(
         functools.partial(chain_kernel, n, dims),
         out_shape=jax.ShapeDtypeStruct((kv_local, nq, head_width), bf16),
-        in_specs=[pl.BlockSpec(memory_space=pl.ANY if i == 1 else pltpu.VMEM) for i in range(8)],
+        in_specs=[pl.BlockSpec(memory_space=pltpu.VMEM)] * 8,
         out_specs=pl.BlockSpec(memory_space=pltpu.VMEM),
         scratch_shapes=[
             vm((2, hh, nq + 16, head_width), bf16),

time: 40.4 us -> 40.4 us (level)
  no operation moved by 1% of the time
where the time goes in v6:
time: 40.4 us; the launch traced here: 40 us
  Pallas kernels  36.1 us (89%)
  local copies, waits for them, and re-layouts  2.63 us (7%)
  other arithmetic  1.1 us (3%)
    pallas_call x1, Pallas kernels, per_device_paired(): pl.pallas_call(functools.partial(chain_kernel, n, dims), out_shape=jax.Sh...  36.1 us
    transpose x1, other arithmetic, per_device_paired(): vx = vx.transpose(0, 2, 1).reshape(2, hh, head_width, tokens + 128)  1.1 us

profile of v6, /device:TPU:1, one launch (start us, length us, event | category | flops | bytes accessed | tf_op | source)
XLA Modules:
  0.0 40.0 jit_solution(13418665830388424411)
XLA Ops:
  0.0 0.8 %copy_bitcast_fusion.1 = (bf16[4,32,128]{2,1,0:T(8,128)(2,1)S(1)}, bf16[4,32,128]{2,1,0:T(8,128)(2,1)S(1)}) fusion(bf16[4,4,8,128]{3,0,2,1:T(4,128)(2,1)} %bitcast.31, bf16[4,4,8,128]{3,0,2,1:T(4,128)(2,1)} %bitcast.32), kind=kLoop, calls=%fused_computation.5 | loop fusion | bytes 131072 | tf_op jit(solution)/shard_map/reshape | solution.py:568
  0.8 1.1 %fusion.2 = bf16[4,128,640]{1,2,0:T(8,128)(2,1)S(1)} fusion(bf16[4,4,128]{2,1,0:T(4,128)(2,1)} %param.15, bf16[4,512,128]{2,1,0:T(8,128)(2,1)} %param.13), kind=kLoop, calls=%fused_computation.3 | loop fusion | flops 1966080 | bytes 1183744 | tf_op jit(solution)/shard_map/transpose | solution.py:566
  1.9 0.0 copy-start.1
  1.9 0.0 copy-start.2
  1.9 0.0 copy-start.3
  1.9 0.0 copy-start.4
  1.9 0.0 copy-start
  2.0 0.3 copy.11
  2.3 0.6 %copy-done.1 = bf16[4,8,32,128]{3,2,1,0:T(8,128)(2,1)S(1)} copy-done((bf16[4,8,32,128]{3,2,1,0:T(8,128)(2,1)S(1)}, bf16[4,8,32,128]{3,2,1,0:T(8,128)(2,1)}, u32[]{:S(2)}) %copy-start.1) | copy-done | bytes 262168
  2.9 0.1 copy.10
  2.9 0.0 copy-done.2
  3.0 0.0 copy-done.3
  3.0 0.0 copy-done.4
  3.0 0.1 pad.19
  3.1 0.0 copy-done
  3.1 36.1 %shard_map.91 = bf16[4,256,128]{2,1,0:T(8,128)(2,1)S(1)} custom-call(bf16[4,256,128]{2,1,0:T(8,128)(2,1)S(1)} %bitcast.25, bf16[4,512,128]{2,1,0:T(8,128)(2,1)S(1)} %copy-done, bf16[2,2,16,128]{3,2,1,0:T(8,128)(2,1)S(1)} %bitcast.27, bf16[2,2,128,640]{3,2,1,0:T(8,128)(2,1)S(1)} %bitcast.24, s32[4,16,16]{2,1,0:T(8,128)S(1)} %pad.18.picks, ...), custom_call_target="tpu_custom_call" | custom-call | flops 4294967296 | bytes 8388608 | tf_op jit(solution)/shard_map/pallas_call | solution.py:573
  39.2 0.7 %copy.20 = bf16[4,8,4,8,128]{4,3,2,1,0:T(8,128)(2,1)} copy(bf16[4,8,4,8,128]{4,3,1,0,2:T(8,128)(2,1)S(1)} %bitcast.26) | data formatting | bytes 524288 | tf_op jit(solution)/shard_map/transpose | solution.py:621
  (3 shorter events, 0.0 us)
Async XLA Ops:
  1.9 1.0 %copy-start.1 = (bf16[4,8,32,128]{3,2,1,0:T(8,128)(2,1)S(1)}, bf16[4,8,32,128]{3,2,1,0:T(8,128)(2,1)}, u32[]{:S(2)}) copy-start(bf16[4,8,32,128]{3,2,1,0:T(8,128)(2,1)} %param.9) | copy-start | bytes 786436
  1.9 1.0 %copy-start.2 = (s32[8,4,16]{2,1,0:T(4,128)S(1)}, s32[8,4,16]{2,1,0:T(4,128)}, u32[]{:S(2)}) copy-start(s32[8,4,16]{2,1,0:T(4,128)} %param.17) | copy-start | bytes 6148
  1.9 1.0 %copy-start.3 = (bf16[4,4,128]{2,1,0:T(4,128)(2,1)S(1)}, bf16[4,4,128]{2,1,0:T(4,128)(2,1)}, u32[]{:S(2)}) copy-start(bf16[4,4,128]{2,1,0:T(4,128)(2,1)} %param.14) | copy-start | bytes 12292
  1.9 1.0 %copy-start.4 = (s32[4,32]{1,0:T(4,128)S(1)}, s32[4,32]{1,0:T(4,128)}, u32[]{:S(2)}) copy-start(s32[4,32]{1,0:T(4,128)} %param.16) | copy-start | bytes 1540
  1.9 1.1 %copy-start = (bf16[4,512,128]{2,1,0:T(8,128)(2,1)S(1)}, bf16[4,512,128]{2,1,0:T(8,128)(2,1)}, u32[]{:S(2)}) copy-start(bf16[4,512,128]{2,1,0:T(8,128)(2,1)} %keys.1) | copy-start | bytes 1572868
